TPU v7x, 32 devices: a whole 2x2x4 slice. The times are simulated.
32 devices in a mesh: seq: 8 (over y, x, core), tp: 4 (over z).
Axes of the slice: x: 2, y: 2, z: 4, core: 2. Of those that a mesh axis runs over, the one named last changes fastest.
Arguments:
- queries: bfloat16 [12288, 4096], P(('seq', 'tp')), may hold values from -9 to 9
- keys_values: bfloat16 [12288, 2048], P(('seq', 'tp')), may hold values from -8 to 8
- doc_lengths: int32 [8], replicated, may hold values from 1 to 3072, 12288 in all
- block_target: int32 [96], replicated, may hold values from 0 to 7, as said below
Outputs:
- attention_output: bfloat16 [12288, 4096], P('seq', 'tp')
Inputs may be any that keep to these rules, and one draw needn't show every extreme that they name: `doc_lengths`: the lengths add up to 12288, and the largest is exactly 3072. `block_target`: every shard of seq is named by exactly 12 blocks, and the 12 blocks of one shard of seq (blocks k * 12 to k * 12 + 11) name no shard more than 2 times, some shard exactly 2 times.
All inputs are finite; a program needn't handle non-finite values.
Results may differ from a plain program's by a relative error of at most 0.0036.
Values may be sent and summed in bfloat16 or wider, within the bound.
No kernel may reach another device: no remote copies, remote signals or barrier semaphores. Data moves between devices by JAX's collectives and lax.ppermute only.
A program may use at most 128 MiB of HBM per device.

v0:
```python
import math

import jax
import jax.numpy as jnp
from jax import lax
from jax.sharding import PartitionSpec as P

HEADS = 32
KV_HEADS = 8
HEAD = 128
BLOCK = 128
MAXDOC = 3072


floor_score = -1e30


def document_of(starts, positions):
    return jnp.sum((positions[..., None] >= starts).astype(jnp.int32), axis=-1) - 1


def fold_keys(
    fold_state, key_piece, piece_start, query_blocks, query_firsts, starts, tile_rows, tile_count
):
    blocks_here = query_blocks.shape[0]
    block_rows = query_blocks.shape[1]
    kv_heads = query_blocks.shape[2]
    head_size = query_blocks.shape[4]
    piece_rows = key_piece.shape[0]
    slice_rows = min(tile_rows, piece_rows)
    key_pairs = key_piece.reshape(piece_rows, kv_heads, 2, head_size)
    factor = 1.0 / math.sqrt(head_size)
    query_offsets = jnp.arange(block_rows, dtype=jnp.int32)
    slice_offsets = jnp.arange(slice_rows, dtype=jnp.int32)

    def per_block(block_index, block_carry):
        running_max, running_sum, accumulator = block_carry
        query_first = lax.dynamic_index_in_dim(query_firsts, block_index, 0, keepdims=False)
        query_rows = lax.dynamic_index_in_dim(query_blocks, block_index, 0, keepdims=False)
        query_pos = query_first + query_offsets
        query_doc = document_of(starts, query_pos)
        first_tile = (query_first // tile_rows - tile_count + 1) * tile_rows
        block_state = (
            lax.dynamic_index_in_dim(running_max, block_index, 0, keepdims=False),
            lax.dynamic_index_in_dim(running_sum, block_index, 0, keepdims=False),
            lax.dynamic_index_in_dim(accumulator, block_index, 0, keepdims=False),
        )

        def per_tile(tile_index, tile_state):
            key_first = first_tile + tile_index * tile_rows
            key_last = jnp.minimum(key_first + tile_rows - 1, query_first)
            active = document_of(starts, key_last) == query_doc[0]
            active = (
                active
                & (key_first < piece_start + piece_rows)
                & (key_first + tile_rows > piece_start)
            )

            def compute(inner_state):
                block_max, block_sum, block_acc = inner_state
                offset = jnp.clip(key_first, 0, piece_rows - slice_rows)
                chosen = lax.dynamic_slice_in_dim(key_pairs, offset, slice_rows, 0)
                key_pos = offset + slice_offsets
                key_doc = document_of(starts, key_pos)
                allowed = (key_doc[None, :] == query_doc[:, None]) & (
                    key_pos[None, :] <= query_pos[:, None]
                )
                allowed = (
                    allowed
                    & (key_pos[None, :] >= key_first)
                    & (key_pos[None, :] < key_first + tile_rows)
                )
                scores = (
                    jnp.einsum(
                        "qhgd,khd->hgqk",
                        query_rows,
                        chosen[:, :, 0],
                        preferred_element_type=jnp.float32,
                    )
                    * factor
                )
                scores = jnp.where(allowed, scores, floor_score)
                new_max = jnp.maximum(block_max, jnp.max(scores, axis=-1))
                shrink = jnp.exp(block_max - new_max)
                weights = jnp.where(allowed, jnp.exp(scores - new_max[..., None]), 0.0)
                new_sum = block_sum * shrink + jnp.sum(weights, axis=-1)
                new_acc = block_acc * shrink[..., None] + jnp.einsum(
                    "hgqk,khd->hgqd",
                    weights.astype(jnp.bfloat16),
                    chosen[:, :, 1],
                    preferred_element_type=jnp.float32,
                )
                return (new_max, new_sum, new_acc)

            return lax.cond(active, compute, lambda unchanged: unchanged, tile_state)

        block_state = lax.fori_loop(0, tile_count, per_tile, block_state)
        running_max = lax.dynamic_update_index_in_dim(running_max, block_state[0], block_index, 0)
        running_sum = lax.dynamic_update_index_in_dim(running_sum, block_state[1], block_index, 0)
        accumulator = lax.dynamic_update_index_in_dim(accumulator, block_state[2], block_index, 0)
        return (running_max, running_sum, accumulator)

    return lax.fori_loop(0, blocks_here, per_block, fold_state)


def normalize(fold_state):
    running_max, running_sum, accumulator = fold_state
    result = accumulator / running_sum[..., None]
    blocks_here, kv_heads, head_group, block_rows, head_size = result.shape
    result = jnp.transpose(result, (0, 3, 1, 2, 4))
    return result.reshape(blocks_here, block_rows, kv_heads * head_group * head_size).astype(
        jnp.bfloat16
    )


def pack_blocks(send_hot, block_data):
    return jnp.einsum(
        "pk,kbw->pbw", send_hot, block_data, preferred_element_type=jnp.float32
    ).astype(jnp.bfloat16)


def unpack_blocks(receive_hot, received):
    return jnp.einsum(
        "sp,pbw->sbw", receive_hot, received, preferred_element_type=jnp.float32
    ).astype(jnp.bfloat16)


def body(queries, keys_values, doc_lengths, block_target):
    query_local, pair_local = (
        lax.all_to_all(queries, "tp", split_axis=1, concat_axis=0, tiled=True),
        lax.all_to_all(keys_values, "tp", split_axis=1, concat_axis=0, tiled=True),
    )
    token_rows = query_local.shape[0]
    block_rows = BLOCK
    blocks_here = token_rows // block_rows
    kv_heads = pair_local.shape[1] // (2 * HEAD)
    head_group = HEADS // KV_HEADS
    row_width = query_local.shape[1]
    shard_count = lax.axis_size("seq")
    shard_index = lax.axis_index("seq")
    total_blocks = block_target.shape[0]
    per_peer = (blocks_here + shard_count - 1) // shard_count
    slot_total = shard_count * per_peer
    starts = jnp.cumsum(doc_lengths) - doc_lengths
    tile_rows = 4 * BLOCK
    tile_count = MAXDOC // tile_rows + 1
    send_slots = jnp.arange(slot_total, dtype=jnp.int32)
    slot_ids = jnp.arange(blocks_here, dtype=jnp.int32)
    local_targets = lax.dynamic_slice_in_dim(block_target, shard_index * blocks_here, blocks_here)
    earlier_same = (local_targets[None, :] == local_targets[:, None]) & (
        slot_ids[None, :] < slot_ids[:, None]
    )
    send_rank = jnp.sum(earlier_same.astype(jnp.int32), axis=1)
    send_slot = local_targets * per_peer + send_rank
    send_hot = (send_slot[None, :] == send_slots[:, None]).astype(jnp.bfloat16)
    owned = (block_target == shard_index).astype(jnp.int32)
    slot_rank = jnp.cumsum(owned) - owned
    picked = (owned[None, :] == 1) & (slot_rank[None, :] == slot_ids[:, None])
    slot_block = jnp.sum(
        jnp.where(picked, jnp.arange(total_blocks, dtype=jnp.int32)[None, :], 0), axis=1
    )
    source_shard = slot_block // blocks_here
    source_rank = jnp.take(slot_rank, slot_block) - jnp.take(slot_rank, source_shard * blocks_here)
    receive_slot = source_shard * per_peer + source_rank
    receive_hot = (receive_slot[:, None] == send_slots[None, :]).astype(jnp.bfloat16)
    start_state = (
        jnp.full((blocks_here, kv_heads, head_group, block_rows), floor_score, jnp.float32),
        jnp.zeros((blocks_here, kv_heads, head_group, block_rows), jnp.float32),
        jnp.zeros((blocks_here, kv_heads, head_group, block_rows, HEAD), jnp.float32),
    )
    outgoing = pack_blocks(send_hot, query_local.reshape(blocks_here, block_rows, row_width))
    received = lax.all_to_all(outgoing, "seq", split_axis=0, concat_axis=0, tiled=True)
    arrived = unpack_blocks(receive_hot, received).reshape(
        blocks_here, block_rows, kv_heads, head_group, HEAD
    )
    query_firsts = slot_block * block_rows
    fold_state = fold_keys(
        start_state,
        lax.all_gather(pair_local, "seq", axis=0, tiled=True),
        jnp.int32(0),
        arrived,
        query_firsts,
        starts,
        tile_rows,
        tile_count,
    )
    return normalize(fold_state).reshape(token_rows, row_width)


def solution(mesh):
    placed = (P(("seq", "tp"), None), P(("seq", "tp"), None), P(), P())
    return jax.shard_map(
        body, mesh=mesh, in_specs=placed, out_specs=P("seq", "tp"), check_vma=False
    )
```

profile of v0, /device:TPU:3, one launch (start us, length us, event | category | flops | bytes accessed | tf_op | source)
XLA Modules:
  0.0 707.3 jit_solution(12326338333148573742)
XLA Ops:
  8.4 40.5 %all_to_all.40 = bf16[384,4,512]{0,2,1:T(8,128)(2,1)S(1)} all-to-all(bf16[384,4,512]{0,2,1:T(8,128)(2,1)S(1)} %bitcast.98), channel_id=1, replica_groups=mesh['seq'=8,'tp'=4] {'tp'}, dimensions={1} | all-to-all | bytes 3145728 | tf_op jit(solution)/shard_map/all_to_all | solution.py:131
  50.6 4.6 copy.44
  59.5 69.8 %all-to-all-done = bf16[384,4,1024]{0,2,1:T(8,128)(2,1)S(1)} async-done(((bf16[384,4,1024]{0,2,1:T(8,128)(2,1)}), bf16[384,4,1024]{0,2,1:T(8,128)(2,1)S(1)}, u32[]{:S(2)}, u32[]{:S(2)}) %all-to-all-start) | async-done | bytes 3145760 | tf_op jit(solution)/shard_map/all_to_all | solution.py:130
  140.9 6.2 all-to-all-start.1
  149.2 45.6 %all-to-all-done.1 = bf16[16,128,1024]{2,1,0:T(8,128)(2,1)} async-done(((bf16[16,128,1024]{2,1,0:T(8,128)(2,1)}), bf16[16,128,1024]{2,1,0:T(8,128)(2,1)}, u32[]{:S(2)}, u32[]{:S(2)}) %all-to-all-start.1) | async-done | bytes 4194336 | tf_op jit(solution)/shard_map/all_to_all | solution.py:172
  194.8 7.1 %fusion.27 = bf16[12,128,1024]{2,0,1:T(8,128)(2,1)} fusion(bf16[16,128,1024]{2,1,0:T(8,128)(2,1)} %all-to-all-done.1, s32[12]{0:T(128)S(1)} %get-tuple-element.924), kind=kOutput, calls=%fused_computation.49 | convolution fusion | flops 51904704 | bytes 7340080 | tf_op jit(solution)/shard_map/sp,pbw->sbw/dot_general | solution.py:123
  201.9 6.3 copy.49
  208.3 16.6 %copy.52 = bf16[12288,512]{0,1:T(8,128)(2,1)} copy(bf16[12288,512]{1,0:T(8,128)(2,1)} %all-gather.2.cloned.1.call-done) | data formatting | bytes 25165824 | tf_op jit(solution)/shard_map/all_gather | solution.py:179
  224.9 16.6 %copy.54 = bf16[12288,2,2,128]{3,0,1,2:T(8,128)(2,1)} copy(bf16[12288,2,2,128]{0,3,2,1:T(8,128)(2,1)} %bitcast.88) | data formatting | bytes 25165824
  244.9 444.8 %while.92 = (s32[]{:T(128)}, f32[12,2,4,128]{3,2,1,0:T(4,128)S(1)}, f32[12,2,4,128]{3,2,1,0:T(4,128)S(1)}, f32[12,2,4,128,128]{4,3,2,1,0:T(8,128)}, s32[12]{0:T(...) while((s32[]{:T(128)}, f32[12,2,4,128]{3,2,1,0:T(4,128)S(1)}, ...), condition=%wide.region_14.16_spmd.clone, body=%wide.region_4.15_spmd.clone.sunk | while | flops 275860160 | bytes 11659902 | solution.py:103
  251.0 18.4 %while.93 = (s32[]{:T(128)}, f32[2,4,128]{2,1,0:T(4,128)S(1)}, f32[2,4,128]{2,1,0:T(4,128)S(1)}, f32[2,4,128,128]{3,2,1,0:T(8,128)S(1)}, s32[]{:T(128)}, /*index...) while((s32[]{:T(128)}, f32[2,4,128]{2,1,0:T(4,128)S(1)}, ...), condition=%wide.region_13.14_spmd, body=%wide.region_6.13_spmd.sunk | while | flops 275856928 | bytes 8476203 | solution.py:97
  264.8 4.5 conditional.2
  276.3 41.1 %while.93 = (s32[]{:T(128)}, f32[2,4,128]{2,1,0:T(4,128)S(1)}, f32[2,4,128]{2,1,0:T(4,128)S(1)}, f32[2,4,128,128]{3,2,1,0:T(8,128)S(1)}, s32[]{:T(128)}, /*index...) while((s32[]{:T(128)}, f32[2,4,128]{2,1,0:T(4,128)S(1)}, ...), condition=%wide.region_13.14_spmd, body=%wide.region_6.13_spmd.sunk | while | flops 275856928 | bytes 8476203 | solution.py:97
  280.3 4.5 conditional.2
  286.8 4.5 conditional.2
  293.3 4.5 conditional.2
  299.8 4.5 conditional.2
  306.3 4.5 conditional.2
  312.9 4.5 conditional.2
  324.4 41.1 %while.93 = (s32[]{:T(128)}, f32[2,4,128]{2,1,0:T(4,128)S(1)}, f32[2,4,128]{2,1,0:T(4,128)S(1)}, f32[2,4,128,128]{3,2,1,0:T(8,128)S(1)}, s32[]{:T(128)}, /*index...) while((s32[]{:T(128)}, f32[2,4,128]{2,1,0:T(4,128)S(1)}, ...), condition=%wide.region_13.14_spmd, body=%wide.region_6.13_spmd.sunk | while | flops 275856928 | bytes 8476203 | solution.py:97
  328.3 4.5 conditional.2
  334.9 4.5 conditional.2
  341.4 4.5 conditional.2
  347.9 4.5 conditional.2
  354.4 4.5 conditional.2
  360.9 4.5 conditional.2
  372.4 18.4 %while.93 = (s32[]{:T(128)}, f32[2,4,128]{2,1,0:T(4,128)S(1)}, f32[2,4,128]{2,1,0:T(4,128)S(1)}, f32[2,4,128,128]{3,2,1,0:T(8,128)S(1)}, s32[]{:T(128)}, /*index...) while((s32[]{:T(128)}, f32[2,4,128]{2,1,0:T(4,128)S(1)}, ...), condition=%wide.region_13.14_spmd, body=%wide.region_6.13_spmd.sunk | while | flops 275856928 | bytes 8476203 | solution.py:97
  386.2 4.5 conditional.2
  397.7 22.9 %while.93 = (s32[]{:T(128)}, f32[2,4,128]{2,1,0:T(4,128)S(1)}, f32[2,4,128]{2,1,0:T(4,128)S(1)}, f32[2,4,128,128]{3,2,1,0:T(8,128)S(1)}, s32[]{:T(128)}, /*index...) while((s32[]{:T(128)}, f32[2,4,128]{2,1,0:T(4,128)S(1)}, ...), condition=%wide.region_13.14_spmd, body=%wide.region_6.13_spmd.sunk | while | flops 275856928 | bytes 8476203 | solution.py:97
  409.6 4.5 conditional.2
  416.1 4.5 conditional.2
  427.6 18.4 %while.93 = (s32[]{:T(128)}, f32[2,4,128]{2,1,0:T(4,128)S(1)}, f32[2,4,128]{2,1,0:T(4,128)S(1)}, f32[2,4,128,128]{3,2,1,0:T(8,128)S(1)}, s32[]{:T(128)}, /*index...) while((s32[]{:T(128)}, f32[2,4,128]{2,1,0:T(4,128)S(1)}, ...), condition=%wide.region_13.14_spmd, body=%wide.region_6.13_spmd.sunk | while | flops 275856928 | bytes 8476203 | solution.py:97
  441.5 4.5 conditional.2
  453.0 22.9 %while.93 = (s32[]{:T(128)}, f32[2,4,128]{2,1,0:T(4,128)S(1)}, f32[2,4,128]{2,1,0:T(4,128)S(1)}, f32[2,4,128,128]{3,2,1,0:T(8,128)S(1)}, s32[]{:T(128)}, /*index...) while((s32[]{:T(128)}, f32[2,4,128]{2,1,0:T(4,128)S(1)}, ...), condition=%wide.region_13.14_spmd, body=%wide.region_6.13_spmd.sunk | while | flops 275856928 | bytes 8476203 | solution.py:97
  464.9 4.5 conditional.2
  471.4 4.5 conditional.2
  482.8 36.5 %while.93 = (s32[]{:T(128)}, f32[2,4,128]{2,1,0:T(4,128)S(1)}, f32[2,4,128]{2,1,0:T(4,128)S(1)}, f32[2,4,128,128]{3,2,1,0:T(8,128)S(1)}, s32[]{:T(128)}, /*index...) while((s32[]{:T(128)}, f32[2,4,128]{2,1,0:T(4,128)S(1)}, ...), condition=%wide.region_13.14_spmd, body=%wide.region_6.13_spmd.sunk | while | flops 275856928 | bytes 8476203 | solution.py:97
  488.8 4.5 conditional.2
  495.3 4.5 conditional.2
  501.8 4.5 conditional.2
  508.3 4.5 conditional.2
  514.8 4.5 conditional.2
  526.3 41.1 %while.93 = (s32[]{:T(128)}, f32[2,4,128]{2,1,0:T(4,128)S(1)}, f32[2,4,128]{2,1,0:T(4,128)S(1)}, f32[2,4,128,128]{3,2,1,0:T(8,128)S(1)}, s32[]{:T(128)}, /*index...) while((s32[]{:T(128)}, f32[2,4,128]{2,1,0:T(4,128)S(1)}, ...), condition=%wide.region_13.14_spmd, body=%wide.region_6.13_spmd.sunk | while | flops 275856928 | bytes 8476203 | solution.py:97
  530.3 4.5 conditional.2
  536.8 4.5 conditional.2
  543.3 4.5 conditional.2
  549.8 4.5 conditional.2
  556.3 4.5 conditional.2
  562.8 4.5 conditional.2
  574.3 45.6 %while.93 = (s32[]{:T(128)}, f32[2,4,128]{2,1,0:T(4,128)S(1)}, f32[2,4,128]{2,1,0:T(4,128)S(1)}, f32[2,4,128,128]{3,2,1,0:T(8,128)S(1)}, s32[]{:T(128)}, /*index...) while((s32[]{:T(128)}, f32[2,4,128]{2,1,0:T(4,128)S(1)}, ...), condition=%wide.region_13.14_spmd, body=%wide.region_6.13_spmd.sunk | while | flops 275856928 | bytes 8476203 | solution.py:97
  576.3 4.5 conditional.2
  582.8 4.5 conditional.2
  589.3 4.5 conditional.2
  595.8 4.5 conditional.2
  602.3 4.5 conditional.2
  608.9 4.5 conditional.2
  615.4 4.5 conditional.2
  626.9 32.0 %while.93 = (s32[]{:T(128)}, f32[2,4,128]{2,1,0:T(4,128)S(1)}, f32[2,4,128]{2,1,0:T(4,128)S(1)}, f32[2,4,128,128]{3,2,1,0:T(8,128)S(1)}, s32[]{:T(128)}, /*index...) while((s32[]{:T(128)}, f32[2,4,128]{2,1,0:T(4,128)S(1)}, ...), condition=%wide.region_13.14_spmd, body=%wide.region_6.13_spmd.sunk | while | flops 275856928 | bytes 8476203 | solution.py:97
  634.8 4.5 conditional.2
  641.3 4.5 conditional.2
  647.8 4.5 conditional.2
  654.3 4.5 conditional.2
  665.8 22.9 %while.93 = (s32[]{:T(128)}, f32[2,4,128]{2,1,0:T(4,128)S(1)}, f32[2,4,128]{2,1,0:T(4,128)S(1)}, f32[2,4,128,128]{3,2,1,0:T(8,128)S(1)}, s32[]{:T(128)}, /*index...) while((s32[]{:T(128)}, f32[2,4,128]{2,1,0:T(4,128)S(1)}, ...), condition=%wide.region_13.14_spmd, body=%wide.region_6.13_spmd.sunk | while | flops 275856928 | bytes 8476203 | solution.py:97
  677.7 4.5 conditional.2
  (780 shorter events, 340.3 us)
Async XLA Ops:
  6.5 201.7 %all-gather.2.cloned.1.call-start = ((), (), s32[]{:S(2)}) async-start(), calls=%async_computation.3 | async-start | bytes 14155776 | tf_op jit(solution)/shard_map/all_gather | solution.py:179
  55.2 4.0 copy-start.1
  55.2 74.1 %all-to-all-start = ((bf16[384,4,1024]{0,2,1:T(8,128)(2,1)}), bf16[384,4,1024]{0,2,1:T(8,128)(2,1)S(1)}, u32[]{:S(2)}, u32[]{:S(2)}) async-start(bf16[384,4,1024]{0,2,1:T(8,128)(2,1)} %bitcast.93), calls=%async_computation | async-start | bytes 6291456 | tf_op jit(solution)/shard_map/all_to_all | solution.py:130
  129.3 1.7 copy-start
  140.9 6.2 copy-start.2
  140.9 53.9 %all-to-all-start.1 = ((bf16[16,128,1024]{2,1,0:T(8,128)(2,1)}), bf16[16,128,1024]{2,1,0:T(8,128)(2,1)}, u32[]{:S(2)}, u32[]{:S(2)}) async-start(bf16[16,128,1024]{2,1,0:T(8,128)(2,1)} %copy.47), calls=%async_computation.1 | async-start | bytes 8388608 | tf_op jit(solution)/shard_map/all_to_all | solution.py:172
Sparse Core Ops, SparseCore 0:
  50.7 72.7 all-gather.1
where the time goes:
time: 715 us; the launch traced here: 707 us
  matrix products  160 us (22%)
  loops' own time  145 us (20%)
  waiting for transfers between devices  115 us (16%)
  local copies, waits for them, and re-layouts  113 us (16%)
  other arithmetic  110 us (15%)
  blocking collectives  40.5 us (6%)
  between operations  13.5 us (2%)
  starting transfers between devices  10.2 us (1%)
    another operation x12, loops' own time, per_block(): block_state = lax.fori_loop(0, tile_count, per_tile, block_state)  111 us
    dot_general x43, matrix products, compute(): jnp.einsum('hgqk,khd->hgqd', weights.astype(jnp.bfloat16), chosen[:, :, 1...  87.9 us
    all_to_all x1, waiting for transfers between devices, body(): lax.all_to_all(queries, 'tp', split_axis=1, concat_axis=0, tiled=True)  69.8 us
    dot_general x43, matrix products, compute(): jnp.einsum('qhgd,khd->hgqk', query_rows, chosen[:, :, 0], preferred_eleme...  62 us
    reduce_sum x139, other arithmetic, document_of(): jnp.sum((positions[..., None] >= starts).astype(jnp.int32), axis=-1) - 1  58.9 us
    all_to_all x1, waiting for transfers between devices, body(): lax.all_to_all(outgoing, 'seq', split_axis=0, concat_axis=0, tiled=True)  45.6 us
    all_to_all x1, blocking collectives, body(): lax.all_to_all(keys_values, 'tp', split_axis=1, concat_axis=0, tiled=True)  40.5 us
    another operation x1, loops' own time, fold_keys(): return lax.fori_loop(0, blocks_here, per_block, fold_state)  30.1 us
  transfers between devices with their start and end apart: 3, of which 2 were waited for; matrix products, arithmetic and copies ran while one was open for 4% of the time, Pallas kernels for 0%

commit v1 on v0

v1 whole, which is shorter than its diff:
```python
import functools
import math

import jax
import jax.numpy as jnp
from jax import lax
from jax.experimental import pallas as pl
from jax.experimental.pallas import tpu as pltpu
from jax.sharding import PartitionSpec as P

HEADS = 32
KV_HEADS = 8
HEAD = 128
BLOCK = 128
MAXDOC = 3072

GROUP = HEADS // KV_HEADS
KEY_TILE = 512
QUERY_TILE = 256
PIECE_HEADS = 2
FLOOR = -1e30
EXP2_SCALE = math.log2(math.e) / math.sqrt(HEAD)

NT = (((1,), (1,)), ((), ()))


def doc_starts(lengths_ref, base):
    starts, total = [], -base
    for doc in range(lengths_ref.shape[0]):
        starts.append(total)
        total = total + lengths_ref[doc]
    return starts


def attend_kernel(
    shard_rows,
    halo,
    per_peer,
    lengths_ref,
    target_ref,
    *refs,
):
    (far_even, far_odd, near, own, query_hbm, out_ref, keys, queries, scores, top, total, acc, sems) = refs
    shard = lax.axis_index("seq")
    odd = lax.rem(shard, 2) == 1
    heads_here = queries.shape[1] // HEAD
    copies = [
        pltpu.make_async_copy(near, keys.at[pl.ds(shard_rows, shard_rows)], sems.at[1]),
        pltpu.make_async_copy(own, keys.at[pl.ds(2 * shard_rows, shard_rows)], sems.at[2]),
        pltpu.make_async_copy(query_hbm, queries, sems.at[3]),
    ]
    for copy in copies:
        copy.start()

    @pl.when(odd)
    def _():
        pltpu.make_async_copy(far_odd, keys.at[pl.ds(0, shard_rows)], sems.at[0]).start()

    @pl.when(jnp.logical_not(odd))
    def _():
        pltpu.make_async_copy(far_even, keys.at[pl.ds(0, shard_rows)], sems.at[0]).start()

    base = (shard - halo) * shard_rows
    starts = doc_starts(lengths_ref, base)

    pltpu.make_async_copy(far_even, keys.at[pl.ds(0, shard_rows)], sems.at[0]).wait()
    for copy in copies:
        copy.wait()

    blocks_here = shard_rows // BLOCK
    tile_blocks = QUERY_TILE // BLOCK
    rows = heads_here * QUERY_TILE
    chunks = KEY_TILE // 128

    def slot_of(block):
        goal = target_ref[shard * blocks_here + block]

        def count(other, rank):
            same = target_ref[shard * blocks_here + other] == goal
            return rank + same.astype(jnp.int32)

        return goal * per_peer + lax.fori_loop(0, block, count, jnp.int32(0))

    def one_tile(tile, carry):
        row_first = pl.multiple_of(tile * QUERY_TILE, QUERY_TILE)
        first = halo * shard_rows + row_first
        last = first + QUERY_TILE - 1
        first_start = starts[0]
        last_start = starts[0]
        for start in starts[1:]:
            first_start = jnp.where(start <= first, start, first_start)
            last_start = jnp.where(start <= last, start, last_start)
        tile_low = lax.div(first_start, KEY_TILE)
        tile_high = lax.div(last, KEY_TILE) + 1
        query = jnp.concatenate(
            [queries[pl.ds(row_first, QUERY_TILE), h * HEAD : (h + 1) * HEAD] for h in range(heads_here)], axis=0
        )
        row_pos = first + lax.broadcasted_iota(jnp.int32, (QUERY_TILE, 1), 0)
        row_start = jnp.full((QUERY_TILE, 1), starts[0], jnp.int32)
        for start in starts[1:]:
            row_start = jnp.where(row_pos >= start, start, row_start)
        top[...] = jnp.full(top.shape, FLOOR, jnp.float32)
        total[...] = jnp.zeros(total.shape, jnp.float32)
        acc[...] = jnp.zeros(acc.shape, jnp.float32)

        def score(index, carry):
            key_first = pl.multiple_of(index * KEY_TILE, KEY_TILE)
            masked = (key_first < last_start) | (key_first + KEY_TILE - 1 > first)
            place = index - tile_low

            def compute(mask):
                found = lax.dot_general(
                    query, keys[pl.ds(key_first, KEY_TILE), 0:HEAD], NT, preferred_element_type=jnp.float32
                )
                if mask:
                    key_pos = key_first + lax.broadcasted_iota(jnp.int32, (QUERY_TILE, KEY_TILE), 1)
                    allowed = (key_pos >= row_start) & (key_pos <= row_pos)
                    bias = jnp.where(allowed, 0.0, FLOOR)
                    found = (found.reshape(heads_here, QUERY_TILE, KEY_TILE) + bias[None]).reshape(rows, KEY_TILE)
                scores[place] = found
                best = top[...]
                for c in range(chunks):
                    best = jnp.maximum(best, found[:, c * 128 : (c + 1) * 128])
                top[...] = best

            @pl.when(masked)
            def _():
                compute(True)

            @pl.when(jnp.logical_not(masked))
            def _():
                compute(False)

            return carry

        lax.fori_loop(tile_low, tile_high, score, 0)
        top[...] = jnp.broadcast_to(jnp.max(top[...], axis=1, keepdims=True), top.shape)

        def weigh(index, carry):
            key_first = pl.multiple_of(index * KEY_TILE, KEY_TILE)
            place = index - tile_low
            best = top[...]
            found = scores[place]
            weights = []
            added = total[...]
            for c in range(chunks):
                weight = jnp.exp2((found[:, c * 128 : (c + 1) * 128] - best) * EXP2_SCALE)
                added = added + weight
                weights.append(weight.astype(jnp.bfloat16))
            total[...] = added
            acc[...] += jnp.dot(
                jnp.concatenate(weights, axis=1),
                keys[pl.ds(key_first, KEY_TILE), HEAD : 2 * HEAD],
                preferred_element_type=jnp.float32,
            )
            return carry

        lax.fori_loop(tile_low, tile_high, weigh, 0)
        result = (acc[...] / jnp.sum(total[...], axis=1, keepdims=True)).astype(jnp.bfloat16)
        for b in range(tile_blocks):
            slot = slot_of(tile * tile_blocks + b)
            for h in range(heads_here):
                low = h * QUERY_TILE + b * BLOCK
                out_ref[slot, :, h * HEAD : (h + 1) * HEAD] = result[low : low + BLOCK]
        return carry

    lax.fori_loop(0, shard_rows // QUERY_TILE, one_tile, 0)


def attend(lengths, target, keys, query, slots, per_peer, halo):
    far_even, far_odd, near, own = keys
    shard_rows, width = query.shape
    rows = (width // HEAD) * QUERY_TILE
    most = (halo * shard_rows) // KEY_TILE + 2
    anywhere = pl.BlockSpec(memory_space=pl.ANY)
    scalars = pl.BlockSpec(memory_space=pltpu.SMEM)
    pairs = shard_rows * 1300 * (width // HEAD)
    return pl.pallas_call(
        functools.partial(attend_kernel, shard_rows, halo, per_peer),
        out_shape=jax.ShapeDtypeStruct((slots, BLOCK, width), jnp.bfloat16),
        in_specs=[scalars, scalars] + [anywhere] * 5,
        out_specs=pl.BlockSpec(memory_space=pltpu.VMEM),
        scratch_shapes=[
            pltpu.VMEM(((halo + 1) * shard_rows, 2 * HEAD), jnp.bfloat16),
            pltpu.VMEM((shard_rows, width), jnp.bfloat16),
            pltpu.VMEM((most, rows, KEY_TILE), jnp.float32),
            pltpu.VMEM((rows, 128), jnp.float32),
            pltpu.VMEM((rows, 128), jnp.float32),
            pltpu.VMEM((rows, HEAD), jnp.float32),
            pltpu.SemaphoreType.DMA((4,)),
        ],
        compiler_params=pltpu.CompilerParams(vmem_limit_bytes=32 << 20),
        cost_estimate=pl.CostEstimate(flops=pairs * 8 * HEAD, bytes_accessed=4 << 20, transcendentals=pairs),
        name="attend",
    )(lengths, target, far_even, far_odd, near, own, query)


def place_kernel(per_peer, column, width, blocks_here, target_ref, *refs):
    received, out_ref, sem = refs[-3], refs[-2], refs[-1]
    shard = lax.axis_index("seq")
    columns = pl.ds(column, width)

    def one(block, carry):
        slot, rank, source, inside = carry
        mine = target_ref[block] == shard

        @pl.when(mine)
        def _():
            pltpu.make_async_copy(
                received.at[source * per_peer + rank],
                out_ref.at[pl.ds(pl.multiple_of(slot * BLOCK, BLOCK), BLOCK), columns],
                sem,
            ).start()

        step = mine.astype(jnp.int32)
        ends = inside == blocks_here - 1
        return (
            slot + step,
            jnp.where(ends, 0, rank + step),
            jnp.where(ends, source + 1, source),
            jnp.where(ends, 0, inside + 1),
        )

    zero = jnp.int32(0)
    lax.fori_loop(0, target_ref.shape[0], one, (zero, zero, zero, zero))
    landed = out_ref.at[:, columns]
    pltpu.make_async_copy(landed, landed, sem).wait()


def place(target, received, out, column, out_shape, per_peer):
    width = received.shape[2]
    anywhere = pl.BlockSpec(memory_space=pl.ANY)
    scalars = pl.BlockSpec(memory_space=pltpu.SMEM)
    before = [] if out is None else [out]
    return pl.pallas_call(
        functools.partial(place_kernel, per_peer, column, width, out_shape[0] // BLOCK),
        out_shape=jax.ShapeDtypeStruct(out_shape, jnp.bfloat16),
        in_specs=[scalars] + [anywhere] * (len(before) + 1),
        out_specs=anywhere,
        scratch_shapes=[pltpu.SemaphoreType.DMA],
        input_output_aliases={1: 0} if before else {},
        name="place",
    )(target, *before, received)


def to_heads(array, tp, piece_width, piece):
    rows = array.shape[0]
    parts = array.reshape(rows, tp, -1, piece_width)[:, :, piece].transpose(1, 0, 2)
    parts = lax.all_to_all(parts, "tp", split_axis=0, concat_axis=0, tiled=True)
    return parts.reshape(tp * rows, piece_width)


def body(queries, keys_values, doc_lengths, block_target):
    tp = lax.axis_size("tp")
    shards = lax.axis_size("seq")
    shard_rows = queries.shape[0] * tp
    blocks_here = shard_rows // BLOCK
    per_peer = (blocks_here + shards - 1) // shards
    slots = shards * per_peer
    halo = (MAXDOC - 1 + shard_rows - 1) // shard_rows
    kv_here = KV_HEADS // tp
    width = PIECE_HEADS * HEAD
    per_kv = GROUP // PIECE_HEADS
    out_shape = (shard_rows, HEADS * HEAD // tp)

    next_shard = [(i, i + 1) for i in range(shards - 1)]
    next_even = [(i, i + 2) for i in range(0, shards - 2, 2)]
    to_odd = [(i, i + 1) for i in range(2, shards, 2)]

    keys = []
    for head in range(kv_here):
        own = to_heads(keys_values, tp, 2 * HEAD, head)
        near = lax.ppermute(own, "seq", next_shard)
        far_even = lax.ppermute(own, "seq", next_even)
        far_odd = lax.ppermute(near, "seq", to_odd)
        keys.append((far_even, far_odd, near, own))

    out = None
    for piece in range(kv_here * per_kv):
        query = to_heads(queries, tp, width, piece)
        sent = attend(doc_lengths, block_target, keys[piece // per_kv], query, slots, per_peer, halo)
        received = lax.all_to_all(sent, "seq", split_axis=0, concat_axis=0, tiled=True)
        out = place(block_target, received, out, piece * width, out_shape, per_peer)
    return out


def solution(mesh):
    placed = (P(("seq", "tp"), None), P(("seq", "tp"), None), P(), P())
    return jax.shard_map(
        body, mesh=mesh, in_specs=placed, out_specs=P("seq", "tp"), check_vma=False
    )
```

time: 715 us -> 373 us (0.52)
  the two profiles are of different devices: /device:TPU:3 before, /device:TPU:0 now
where the time goes in v1:
time: 373 us; the launch traced here: 371 us
  Pallas kernels  157 us (42%)
  starting transfers between devices  90.5 us (24%)
  waiting for transfers between devices  82.5 us (22%)
  local copies, waits for them, and re-layouts  41.1 us (11%)
    pallas_call x4, Pallas kernels, place(): pl.pallas_call(functools.partial(place_kernel, per_peer, column, width, o...  103 us
    all_to_all x6, waiting for transfers between devices, to_heads(): parts = lax.all_to_all(parts, 'tp', split_axis=0, concat_axis=0, tiled=True)  68.2 us
    pallas_call x4, Pallas kernels, attend(): pl.pallas_call(functools.partial(attend_kernel, shard_rows, halo, per_pee...  54 us
    all_to_all x4, starting transfers between devices, body(): lax.all_to_all(sent, 'seq', split_axis=0, concat_axis=0, tiled=True)  50.4 us
    all_to_all x6, starting transfers between devices, to_heads(): parts = lax.all_to_all(parts, 'tp', split_axis=0, concat_axis=0, tiled=True)  25.2 us
    unnamed x26, local copies, waits for them, and re-layouts  17.2 us
    slice x2, local copies, waits for them, and re-layouts, to_heads(): array.reshape(rows, tp, -1, piece_width)[:, :, piece].transpose(1, 0, 2)  15 us
    ppermute x2, waiting for transfers between devices, body(): far_even = lax.ppermute(own, 'seq', next_even)  10.7 us
  transfers between devices with their start and end apart: 16, of which 8 were waited for; matrix products, arithmetic and copies ran while one was open for 8% of the time, Pallas kernels for 35%

profile of v1, /device:TPU:0, one launch (start us, length us, event | category | flops | bytes accessed | tf_op | source)
XLA Modules:
  0.0 370.9 jit_solution(2959635162091003115)
XLA Ops:
  0.0 2.9 reshape.28
  2.9 3.1 fusion.1
  5.9 1.1 copy.31
  7.1 6.3 %all-to-all-start = ((bf16[4,384,256]{2,1,0:T(8,128)(2,1)}), bf16[4,384,256]{2,1,0:T(8,128)(2,1)S(1)}, u32[]{:S(2)}, u32[]{:S(2)}) async-start(bf16[4,384,256]{2,1,0:T(8,128)(2,1)} %bitcast.35), calls=%async_computation | async-start | bytes 1572864 | tf_op jit(solution)/shard_map/all_to_all | solution.py:249
  13.4 6.2 %reshape.30 = bf16[384,4,4,256]{3,2,1,0:T(4,128)(2,1)} reshape(bf16[384,4096]{1,0:T(8,128)(2,1)} %param.4) | data formatting | bytes 6291456 | tf_op jit(solution)/shard_map/reshape | solution.py:248
  19.5 11.9 %fusion = (bf16[384,4,1,256]{3,2,1,0:T(2,128)(2,1)}, bf16[384,4,1,256]{3,2,1,0:T(2,128)(2,1)}, bf16[384,4,1,256]{3,2,1,0:T(2,128)(2,1)S(1)}, bf16[384,4,1,256]{3,2,1,0:T(2,128)(2,1)S(1)}) fusion(bf16[384,4,4,256]{3,2,1,0:T(4,128)(2,1)} %reshape.30), kind=kLoop, calls=%fused_computation.6 | loop fusion | bytes 6291456 | tf_op jit(solution)/shard_map/slice | solution.py:248
  31.4 1.1 copy.29
  32.6 0.9 all-to-all-done
  33.5 4.2 %all-to-all-start.3 = ((bf16[4,384,256]{2,1,0:T(8,128)(2,1)}), bf16[4,384,256]{2,1,0:T(8,128)(2,1)S(1)}, u32[]{:S(2)}, u32[]{:S(2)}) async-start(bf16[4,384,256]{2,1,0:T(8,128)(2,1)} %bitcast.50), calls=%async_computation.3 | async-start | bytes 1572864 | tf_op jit(solution)/shard_map/all_to_all | solution.py:249
  37.7 1.1 copy.30
  38.8 18.4 %all-to-all-done.3 = bf16[4,384,256]{2,1,0:T(8,128)(2,1)S(1)} async-done(((bf16[4,384,256]{2,1,0:T(8,128)(2,1)}), bf16[4,384,256]{2,1,0:T(8,128)(2,1)S(1)}, u32[]{:S(2)}, u32[]{:S(2)}) %all-to-all-start.3) | async-done | bytes 786464 | tf_op jit(solution)/shard_map/all_to_all | solution.py:249
  57.2 0.0 copy-start
  57.2 3.5 all-to-all-start.1
  60.7 2.5 copy.28
  63.2 0.0 copy-done
  63.2 17.0 %all-to-all-done.1 = bf16[4,384,256]{2,1,0:T(8,128)(2,1)S(1)} async-done(((bf16[4,384,256]{2,1,0:T(8,128)(2,1)}), bf16[4,384,256]{2,1,0:T(8,128)(2,1)S(1)}, u32[]{:S(2)}, u32[]{:S(2)}) %all-to-all-start.1) | async-done | bytes 786464 | tf_op jit(solution)/shard_map/all_to_all | solution.py:249
  80.3 3.5 all-to-all-start.5
  83.8 2.5 copy.27
  86.3 17.0 %all-to-all-done.5 = bf16[4,384,256]{2,1,0:T(8,128)(2,1)S(1)} async-done(((bf16[4,384,256]{2,1,0:T(8,128)(2,1)}), bf16[4,384,256]{2,1,0:T(8,128)(2,1)S(1)}, u32[]{:S(2)}, u32[]{:S(2)}) %all-to-all-start.5) | async-done | bytes 786464 | tf_op jit(solution)/shard_map/all_to_all | solution.py:249
  103.3 3.5 all-to-all-start.6
  106.8 2.2 collective-permute-start.1
  109.0 0.0 copy-start.2
  109.0 2.6 copy.26
  111.6 14.8 %all-to-all-done.6 = bf16[4,384,256]{2,1,0:T(8,128)(2,1)S(1)} async-done(((bf16[4,384,256]{2,1,0:T(8,128)(2,1)}), bf16[4,384,256]{2,1,0:T(8,128)(2,1)S(1)}, u32[]{:S(2)}, u32[]{:S(2)}) %all-to-all-start.6) | async-done | bytes 786464 | tf_op jit(solution)/shard_map/all_to_all | solution.py:249
  126.4 4.2 %all-to-all-start.8 = ((bf16[4,384,256]{2,1,0:T(8,128)(2,1)}), bf16[4,384,256]{2,1,0:T(8,128)(2,1)}, u32[]{:S(2)}, u32[]{:S(2)}) async-start(bf16[4,384,256]{2,1,0:T(8,128)(2,1)} %bitcast.47), calls=%async_computation.8 | async-start | bytes 1572864 | tf_op jit(solution)/shard_map/all_to_all | solution.py:249
  130.6 3.4 collective-permute-start
  134.1 0.0 collective-permute-done.1.refs_2_
  134.1 0.7 collective-permute-start.2
  134.8 2.2 collective-permute-start.4
  137.0 10.7 %collective-permute-done.refs_0_ = bf16[1536,256]{1,0:T(8,128)(2,1)S(1)} collective-permute-done((bf16[1536,256]{1,0:T(8,128)(2,1)S(1)}, bf16[1536,256]{1,0:T(8,128)(2,1)S(1)}, u32[]{:S(2)}, u32[]{:S(2)}) %collective-permute-start) | collective-permute-done | bytes 786464 | tf_op jit(solution)/shard_map/ppermute | solution.py:274
  147.7 0.0 collective-permute-done.2.refs_1_
  147.7 0.0 copy-done.2
  147.7 0.0 copy-done.7
  147.7 1.1 copy-done.1
  148.8 13.3 %attend.5 = bf16[16,128,256]{2,1,0:T(8,128)(2,1)} custom-call(s32[8]{0:T(128)S(1)} %copy-done.7, s32[96]{0:T(128)S(1)} %copy-done.2, bf16[1536,256]{1,0:T(8,128)(2,1)S(1)} %collective-permute-done.refs_0_, bf16[1536,256]{1,0:T(8,128)(2,1)S(1)} %collective-permute-done.2.refs_1_, bf16[1536,256]{1,0:T(8,128)(2,1)} %collective-permute-done.1.refs_2_, ...), custom_call_target="tpu_custom_call" | custom-call | flops 4089446400 | bytes 4194304 | tf_op jit(solution)/shard_map/attend/pallas_call | solution.py:178
  162.2 0.0 copy-start.3
  162.2 0.9 copy-done.3
  163.0 0.9 copy-done.5
  163.9 0.0 all-to-all-done.8
  163.9 12.5 %all-to-all-start.4 = ((bf16[16,128,256]{2,1,0:T(8,128)(2,1)}), bf16[16,128,256]{2,1,0:T(8,128)(2,1)}, u32[]{:S(2)}, u32[]{:S(2)}) async-start(bf16[16,128,256]{2,1,0:T(8,128)(2,1)} %attend.5), calls=%async_computation.4 | async-start | bytes 2097152 | tf_op jit(solution)/shard_map/all_to_all | solution.py:282
  176.5 4.8 %collective-permute-start.3 = (bf16[1536,256]{1,0:T(8,128)(2,1)S(1)}, bf16[1536,256]{1,0:T(8,128)(2,1)}, u32[]{:S(2)}, u32[]{:S(2)}) collective-permute-start(bf16[1536,256]{1,0:T(8,128)(2,1)S(1)} %bitcast.41), channel_id=1, source_target_pairs={{0,8},{8,16},{16,24},{1,9},{9,17},{17,25},{2,10},{10,18},{18,26},{... | collective-permute-start | bytes 2359304 | tf_op jit(solution)/shard_map/ppermute | solution.py:274
  181.3 0.0 collective-permute-done.4.refs_2_
  181.3 1.6 collective-permute-start.5
  182.8 1.1 copy-done.4
  184.0 1.1 copy-done.6
  185.1 13.3 %attend.4 = bf16[16,128,256]{2,1,0:T(8,128)(2,1)} custom-call(s32[8]{0:T(128)S(1)} %copy-done.7, s32[96]{0:T(128)S(1)} %copy-done.2, bf16[1536,256]{1,0:T(8,128)(2,1)S(1)} %copy-done.4, bf16[1536,256]{1,0:T(8,128)(2,1)S(1)} %copy-done.6, bf16[1536,256]{1,0:T(8,128)(2,1)} %collective-permute-done.1.refs_2_, bf16[1536,256]{1,0:T(8,128)(2,1)S(1)} %bitcast.39, ...), custom_call_target="tpu_custom_call" | custom-call | flops 4089446400 | bytes 4194304 | tf_op jit(solution)/shard_map/attend/pallas_call | solution.py:178
  198.4 0.0 all-to-all-done.4.refs_1_
  198.4 10.9 %all-to-all-start.2 = ((bf16[16,128,256]{2,1,0:T(8,128)(2,1)}), bf16[16,128,256]{2,1,0:T(8,128)(2,1)}, u32[]{:S(2)}, u32[]{:S(2)}) async-start(bf16[16,128,256]{2,1,0:T(8,128)(2,1)} %attend.4), calls=%async_computation.2 | async-start | bytes 2097152 | tf_op jit(solution)/shard_map/all_to_all | solution.py:282
  209.3 0.0 collective-permute-done.3.refs_0_
  209.3 0.0 collective-permute-done.5.refs_1_
  209.3 13.6 %attend.6 = bf16[16,128,256]{2,1,0:T(8,128)(2,1)} custom-call(s32[8]{0:T(128)S(1)} %copy-done.7, s32[96]{0:T(128)S(1)} %copy-done.2, bf16[1536,256]{1,0:T(8,128)(2,1)} %collective-permute-done.3.refs_0_, bf16[1536,256]{1,0:T(8,128)(2,1)} %collective-permute-done.5.refs_1_, bf16[1536,256]{1,0:T(8,128)(2,1)} %collective-permute-done.4.refs_2_, ...), custom_call_target="tpu_custom_call" | custom-call | flops 4089446400 | bytes 4194304 | tf_op jit(solution)/shard_map/attend/pallas_call | solution.py:178
  222.9 1.9 all-to-all-done.2.refs_0_
  224.8 13.7 %all-to-all-start.7 = ((bf16[16,128,256]{2,1,0:T(8,128)(2,1)}), bf16[16,128,256]{2,1,0:T(8,128)(2,1)S(1)}, u32[]{:S(2)}, u32[]{:S(2)}) async-start(bf16[16,128,256]{2,1,0:T(8,128)(2,1)} %attend.6), calls=%async_computation.7 | async-start | bytes 2097152 | tf_op jit(solution)/shard_map/all_to_all | solution.py:282
  238.5 13.8 %attend.7 = bf16[16,128,256]{2,1,0:T(8,128)(2,1)} custom-call(s32[8]{0:T(128)S(1)} %copy-done.7, s32[96]{0:T(128)S(1)} %copy-done.2, bf16[1536,256]{1,0:T(8,128)(2,1)} %collective-permute-done.3.refs_0_, bf16[1536,256]{1,0:T(8,128)(2,1)} %collective-permute-done.5.refs_1_, bf16[1536,256]{1,0:T(8,128)(2,1)} %collective-permute-done.4.refs_2_, ...), custom_call_target="tpu_custom_call" | custom-call | flops 4089446400 | bytes 4194304 | tf_op jit(solution)/shard_map/attend/pallas_call | solution.py:178
  252.3 1.6 all-to-all-done.7.refs_1_
  253.9 13.3 %all-to-all-start.9 = ((bf16[16,128,256]{2,1,0:T(8,128)(2,1)}), bf16[16,128,256]{2,1,0:T(8,128)(2,1)S(1)}, u32[]{:S(2)}, u32[]{:S(2)}) async-start(bf16[16,128,256]{2,1,0:T(8,128)(2,1)} %attend.7), calls=%async_computation.9 | async-start | bytes 2097152 | tf_op jit(solution)/shard_map/all_to_all | solution.py:282
  267.2 25.7 %place.4.refs_0_ = bf16[1536,1024]{1,0:T(8,128)(2,1)} custom-call(s32[96]{0:T(128)} %target_ref.15, bf16[16,128,256]{2,1,0:T(8,128)(2,1)} %all-to-all-done.2.refs_0_), custom_call_target="tpu_custom_call" | custom-call | tf_op jit(solution)/shard_map/place/pallas_call | solution.py:235
  292.9 0.0 copy-done.8
  292.9 25.7 %place.5.refs_0_ = bf16[1536,1024]{1,0:T(8,128)(2,1)} custom-call(s32[96]{0:T(128)} %target_ref.15, bf16[1536,1024]{1,0:T(8,128)(2,1)} %place.4.refs_0_, bf16[16,128,256]{2,1,0:T(8,128)(2,1)} %all-to-all-done.4.refs_1_), custom_call_target="tpu_custom_call", output_to_operand_aliasing={{}: (1, {})} | custom-call | tf_op jit(solution)/shard_map/place/pallas_call | solution.py:235
  318.6 25.7 %place.6.refs_0_ = bf16[1536,1024]{1,0:T(8,128)(2,1)} custom-call(s32[96]{0:T(128)} %target_ref.15, bf16[1536,1024]{1,0:T(8,128)(2,1)} %place.5.refs_0_, bf16[16,128,256]{2,1,0:T(8,128)(2,1)} %copy-done.8), custom_call_target="tpu_custom_call", output_to_operand_aliasing={{}: (1, {})} | custom-call | tf_op jit(solution)/shard_map/place/pallas_call | solution.py:235
  344.3 0.0 all-to-all-done.9.refs_1_
  344.3 0.0 copy-start.9
  344.3 1.0 copy-done.9
  345.3 25.7 %place.7 = bf16[1536,1024]{1,0:T(8,128)(2,1)} custom-call(s32[96]{0:T(128)} %target_ref.15, bf16[1536,1024]{1,0:T(8,128)(2,1)} %place.6.refs_0_, bf16[16,128,256]{2,1,0:T(8,128)(2,1)} %copy-done.9), custom_call_target="tpu_custom_call", output_to_operand_aliasing={{}: (1, {})} | custom-call | tf_op jit(solution)/shard_map/place/pallas_call | solution.py:235
  (6 shorter events, 0.0 us)
Async XLA Ops:
  7.1 26.4 %all-to-all-start = ((bf16[4,384,256]{2,1,0:T(8,128)(2,1)}), bf16[4,384,256]{2,1,0:T(8,128)(2,1)S(1)}, u32[]{:S(2)}, u32[]{:S(2)}) async-start(bf16[4,384,256]{2,1,0:T(8,128)(2,1)} %bitcast.35), calls=%async_computation | async-start | bytes 1572864 | tf_op jit(solution)/shard_map/all_to_all | solution.py:249
  33.5 23.7 %all-to-all-start.3 = ((bf16[4,384,256]{2,1,0:T(8,128)(2,1)}), bf16[4,384,256]{2,1,0:T(8,128)(2,1)S(1)}, u32[]{:S(2)}, u32[]{:S(2)}) async-start(bf16[4,384,256]{2,1,0:T(8,128)(2,1)} %bitcast.50), calls=%async_computation.3 | async-start | bytes 1572864 | tf_op jit(solution)/shard_map/all_to_all | solution.py:249
  57.2 6.0 %copy-start = (bf16[4,384,256]{2,1,0:T(8,128)(2,1)}, bf16[4,384,256]{2,1,0:T(8,128)(2,1)S(1)}, u32[]{:S(2)}) copy-start(bf16[4,384,256]{2,1,0:T(8,128)(2,1)S(1)} %all-to-all-done.3) | copy-start | bytes 2359300
  57.2 23.1 %all-to-all-start.1 = ((bf16[4,384,256]{2,1,0:T(8,128)(2,1)}), bf16[4,384,256]{2,1,0:T(8,128)(2,1)S(1)}, u32[]{:S(2)}, u32[]{:S(2)}) async-start(bf16[4,384,256]{2,1,0:T(8,128)(2,1)} %bitcast.49), calls=%async_computation.1 | async-start | bytes 1572864 | tf_op jit(solution)/shard_map/all_to_all | solution.py:249
  80.3 23.1 %all-to-all-start.5 = ((bf16[4,384,256]{2,1,0:T(8,128)(2,1)}), bf16[4,384,256]{2,1,0:T(8,128)(2,1)S(1)}, u32[]{:S(2)}, u32[]{:S(2)}) async-start(bf16[4,384,256]{2,1,0:T(8,128)(2,1)} %bitcast.32), calls=%async_computation.5 | async-start | bytes 1572864 | tf_op jit(solution)/shard_map/all_to_all | solution.py:249
  103.3 23.1 %all-to-all-start.6 = ((bf16[4,384,256]{2,1,0:T(8,128)(2,1)}), bf16[4,384,256]{2,1,0:T(8,128)(2,1)S(1)}, u32[]{:S(2)}, u32[]{:S(2)}) async-start(bf16[4,384,256]{2,1,0:T(8,128)(2,1)} %bitcast.48), calls=%async_computation.6 | async-start | bytes 1572864 | tf_op jit(solution)/shard_map/all_to_all | solution.py:249
  106.8 27.2 %collective-permute-start.1 = (bf16[1536,256]{1,0:T(8,128)(2,1)S(1)}, bf16[1536,256]{1,0:T(8,128)(2,1)}, u32[]{:S(2)}, u32[]{:S(2)}) collective-permute-start(bf16[1536,256]{1,0:T(8,128)(2,1)S(1)} %bitcast.36), channel_id=1, source_target_pairs={{0,4},{4,8},{8,12},{12,16},{16,20},{20,24},{24,28},{1,5},{5,9},{9,... | collective-permute-start | bytes 2359304 | tf_op jit(solution)/shard_map/ppermute | solution.py:273
  109.0 38.7 %copy-start.2 = (s32[96]{0:T(128)S(1)}, s32[96]{0:T(128)}, u32[]{:S(2)}) copy-start(s32[96]{0:T(128)} %target_ref.15) | copy-start | bytes 1156
  109.0 38.7 %copy-start.7 = (s32[8]{0:T(128)S(1)}, s32[8]{0:T(128)}, u32[]{:S(2)}) copy-start(s32[8]{0:T(128)} %lengths_ref.7) | copy-start | bytes 100
  126.4 37.5 %all-to-all-start.8 = ((bf16[4,384,256]{2,1,0:T(8,128)(2,1)}), bf16[4,384,256]{2,1,0:T(8,128)(2,1)}, u32[]{:S(2)}, u32[]{:S(2)}) async-start(bf16[4,384,256]{2,1,0:T(8,128)(2,1)} %bitcast.47), calls=%async_computation.8 | async-start | bytes 1572864 | tf_op jit(solution)/shard_map/all_to_all | solution.py:249
  130.6 17.1 %collective-permute-start = (bf16[1536,256]{1,0:T(8,128)(2,1)S(1)}, bf16[1536,256]{1,0:T(8,128)(2,1)S(1)}, u32[]{:S(2)}, u32[]{:S(2)}) collective-permute-start(bf16[1536,256]{1,0:T(8,128)(2,1)S(1)} %bitcast.37), channel_id=1, source_target_pairs={{0,8},{8,16},{16,24},{1,9},{9,17},{17,25},{2,10},{10,18},{18,26},{... | collective-permute-start | bytes 2359304 | tf_op jit(solution)/shard_map/ppermute | solution.py:274
  134.1 13.6 %collective-permute-start.2 = (bf16[1536,256]{1,0:T(8,128)(2,1)}, bf16[1536,256]{1,0:T(8,128)(2,1)S(1)}, u32[]{:S(2)}, u32[]{:S(2)}) collective-permute-start(bf16[1536,256]{1,0:T(8,128)(2,1)} %collective-permute-done.1.refs_2_), channel_id=1, source_target_pairs={{8,12},{16,20},{24,28},{9,13},{17,21},{25,29},{10,14},{18,22},{26,... | collective-permute-start | bytes 2359304 | tf_op jit(solution)/shard_map/ppermute | solution.py:275
  134.8 46.5 %collective-permute-start.4 = (bf16[1536,256]{1,0:T(8,128)(2,1)S(1)}, bf16[1536,256]{1,0:T(8,128)(2,1)}, u32[]{:S(2)}, u32[]{:S(2)}) collective-permute-start(bf16[1536,256]{1,0:T(8,128)(2,1)S(1)} %bitcast.40), channel_id=1, source_target_pairs={{0,4},{4,8},{8,12},{12,16},{16,20},{20,24},{24,28},{1,5},{5,9},{9,... | collective-permute-start | bytes 2359304 | tf_op jit(solution)/shard_map/ppermute | solution.py:273
  147.7 1.1 copy-start.1
  162.2 0.9 copy-start.3
  163.0 0.9 copy-start.5
  163.9 34.5 %all-to-all-start.4 = ((bf16[16,128,256]{2,1,0:T(8,128)(2,1)}), bf16[16,128,256]{2,1,0:T(8,128)(2,1)}, u32[]{:S(2)}, u32[]{:S(2)}) async-start(bf16[16,128,256]{2,1,0:T(8,128)(2,1)} %attend.5), calls=%async_computation.4 | async-start | bytes 2097152 | tf_op jit(solution)/shard_map/all_to_all | solution.py:282
  176.5 32.9 %collective-permute-start.3 = (bf16[1536,256]{1,0:T(8,128)(2,1)S(1)}, bf16[1536,256]{1,0:T(8,128)(2,1)}, u32[]{:S(2)}, u32[]{:S(2)}) collective-permute-start(bf16[1536,256]{1,0:T(8,128)(2,1)S(1)} %bitcast.41), channel_id=1, source_target_pairs={{0,8},{8,16},{16,24},{1,9},{9,17},{17,25},{2,10},{10,18},{18,26},{... | collective-permute-start | bytes 2359304 | tf_op jit(solution)/shard_map/ppermute | solution.py:274
  181.3 28.1 %collective-permute-start.5 = (bf16[1536,256]{1,0:T(8,128)(2,1)}, bf16[1536,256]{1,0:T(8,128)(2,1)}, u32[]{:S(2)}, u32[]{:S(2)}) collective-permute-start(bf16[1536,256]{1,0:T(8,128)(2,1)} %collective-permute-done.4.refs_2_), channel_id=1, source_target_pairs={{8,12},{16,20},{24,28},{9,13},{17,21},{25,29},{10,14},{18,22},{26,... | collective-permute-start | bytes 2359304 | tf_op jit(solution)/shard_map/ppermute | solution.py:275
  182.8 1.1 copy-start.4
  184.0 1.1 copy-start.6
  198.4 26.4 %all-to-all-start.2 = ((bf16[16,128,256]{2,1,0:T(8,128)(2,1)}), bf16[16,128,256]{2,1,0:T(8,128)(2,1)}, u32[]{:S(2)}, u32[]{:S(2)}) async-start(bf16[16,128,256]{2,1,0:T(8,128)(2,1)} %attend.4), calls=%async_computation.2 | async-start | bytes 2097152 | tf_op jit(solution)/shard_map/all_to_all | solution.py:282
  224.8 29.1 %all-to-all-start.7 = ((bf16[16,128,256]{2,1,0:T(8,128)(2,1)}), bf16[16,128,256]{2,1,0:T(8,128)(2,1)S(1)}, u32[]{:S(2)}, u32[]{:S(2)}) async-start(bf16[16,128,256]{2,1,0:T(8,128)(2,1)} %attend.6), calls=%async_computation.7 | async-start | bytes 2097152 | tf_op jit(solution)/shard_map/all_to_all | solution.py:282
  253.9 39.0 %copy-start.8 = (bf16[16,128,256]{2,1,0:T(8,128)(2,1)}, bf16[16,128,256]{2,1,0:T(8,128)(2,1)S(1)}, u32[]{:S(2)}) copy-start(bf16[16,128,256]{2,1,0:T(8,128)(2,1)S(1)} %all-to-all-done.7.refs_1_) | copy-start | bytes 3145732
  253.9 90.4 %all-to-all-start.9 = ((bf16[16,128,256]{2,1,0:T(8,128)(2,1)}), bf16[16,128,256]{2,1,0:T(8,128)(2,1)S(1)}, u32[]{:S(2)}, u32[]{:S(2)}) async-start(bf16[16,128,256]{2,1,0:T(8,128)(2,1)} %attend.7), calls=%async_computation.9 | async-start | bytes 2097152 | tf_op jit(solution)/shard_map/all_to_all | solution.py:282
  344.3 1.0 copy-start.9

commit v2 on v1

v2 whole, which is shorter than its diff:
```python
import functools
import math

import jax
import jax.numpy as jnp
from jax import lax
from jax.experimental import pallas as pl
from jax.experimental.pallas import tpu as pltpu
from jax.sharding import PartitionSpec as P

HEADS = 32
KV_HEADS = 8
HEAD = 128
BLOCK = 128
MAXDOC = 3072

GROUP = HEADS // KV_HEADS
KEY_TILE = 512
QUERY_TILE = 256
PIECE_HEADS = 2
FLOOR = -1e30
EXP2_SCALE = math.log2(math.e) / math.sqrt(HEAD)
TOTAL_LIMIT = 2.0**64

NT = (((1,), (1,)), ((), ()))

ANYWHERE = pl.BlockSpec(memory_space=pl.ANY)
SCALARS = pl.BlockSpec(memory_space=pltpu.SMEM)


def doc_starts(lengths_ref, base):
    starts, total = [], -base
    for doc in range(lengths_ref.shape[0]):
        starts.append(total)
        total = total + lengths_ref[doc]
    return starts


def attend_kernel(shard_rows, halo, per_peer, sources, *refs):
    lengths_ref, target_ref, far_even, far_odd, near, own = refs[:6]
    query_parts = refs[6 : 6 + sources]
    out_ref, keys, queries, scores, top, total, acc, sems = refs[6 + sources :]
    shard = lax.axis_index("seq")
    me = lax.axis_index("tp")
    odd = lax.rem(shard, 2) == 1
    heads_here = queries.shape[1] // HEAD
    part_rows = shard_rows // sources
    copies = [
        pltpu.make_async_copy(near, keys.at[pl.ds(shard_rows, shard_rows)], sems.at[1]),
        pltpu.make_async_copy(own, keys.at[pl.ds(2 * shard_rows, shard_rows)], sems.at[2]),
    ]
    for x, part in enumerate(query_parts):
        low = pl.multiple_of((me ^ x) * part_rows, part_rows)
        copies.append(pltpu.make_async_copy(part, queries.at[pl.ds(low, part_rows)], sems.at[3 + x]))
    for copy in copies:
        copy.start()

    @pl.when(odd)
    def _():
        pltpu.make_async_copy(far_odd, keys.at[pl.ds(0, shard_rows)], sems.at[0]).start()

    @pl.when(jnp.logical_not(odd))
    def _():
        pltpu.make_async_copy(far_even, keys.at[pl.ds(0, shard_rows)], sems.at[0]).start()

    base = (shard - halo) * shard_rows
    starts = doc_starts(lengths_ref, base)

    pltpu.make_async_copy(far_even, keys.at[pl.ds(0, shard_rows)], sems.at[0]).wait()
    for copy in copies:
        copy.wait()

    blocks_here = shard_rows // BLOCK
    tile_blocks = QUERY_TILE // BLOCK
    rows = heads_here * QUERY_TILE

    def slot_of(block):
        goal = target_ref[shard * blocks_here + block]

        def count(other, rank):
            same = target_ref[shard * blocks_here + other] == goal
            return rank + same.astype(jnp.int32)

        return goal * per_peer + lax.fori_loop(0, block, count, jnp.int32(0))

    def one_tile(tile, carry):
        row_first = pl.multiple_of(tile * QUERY_TILE, QUERY_TILE)
        first = pl.multiple_of(halo * shard_rows + row_first, QUERY_TILE)
        last = first + QUERY_TILE - 1
        first_start = starts[0]
        last_start = starts[0]
        for start in starts[1:]:
            first_start = jnp.where(start <= first, start, first_start)
            last_start = jnp.where(start <= last, start, last_start)
        query = jnp.concatenate(
            [queries[pl.ds(row_first, QUERY_TILE), h * HEAD : (h + 1) * HEAD] for h in range(heads_here)], axis=0
        )
        row_pos = first + lax.broadcasted_iota(jnp.int32, (QUERY_TILE, 1), 0)
        row_start = jnp.full((QUERY_TILE, 1), starts[0], jnp.int32)
        for start in starts[1:]:
            row_start = jnp.where(row_pos >= start, start, row_start)

        def scores_of(key_first, size, mask):
            found = lax.dot_general(
                query, keys[pl.ds(key_first, size), 0:HEAD], NT, preferred_element_type=jnp.float32
            )
            if mask:
                key_pos = key_first + lax.broadcasted_iota(jnp.int32, (QUERY_TILE, size), 1)
                allowed = (key_pos >= row_start) & (key_pos <= row_pos)
                bias = jnp.where(allowed, 0.0, FLOOR)
                found = (found.reshape(heads_here, QUERY_TILE, size) + bias[None]).reshape(rows, size)
            return found

        def fold(found, key_first, size, fresh):
            best = top[...]
            weights = []
            added = None if fresh else total[...]
            for c in range(size // 128):
                weight = jnp.exp2((found[:, c * 128 : (c + 1) * 128] - best) * EXP2_SCALE)
                added = weight if added is None else added + weight
                weights.append(weight.astype(jnp.bfloat16))
            total[...] = added
            product = jnp.dot(
                jnp.concatenate(weights, axis=1),
                keys[pl.ds(key_first, size), HEAD : 2 * HEAD],
                preferred_element_type=jnp.float32,
            )
            acc[...] = product if fresh else acc[...] + product

        def either(masked, run):
            @pl.when(masked)
            def _():
                run(True)

            @pl.when(jnp.logical_not(masked))
            def _():
                run(False)

        def set_top(values):
            top[...] = jnp.broadcast_to(jnp.max(values, axis=1, keepdims=True), top.shape)

        def store():
            result = (acc[...] / jnp.sum(total[...], axis=1, keepdims=True)).astype(jnp.bfloat16)
            for b in range(tile_blocks):
                slot = slot_of(tile * tile_blocks + b)
                for h in range(heads_here):
                    low = h * QUERY_TILE + b * BLOCK
                    out_ref[slot, :, h * HEAD : (h + 1) * HEAD] = result[low : low + BLOCK]

        diagonal = scores_of(first, QUERY_TILE, True)
        set_top(diagonal)
        fold(diagonal, first, QUERY_TILE, True)
        steps = lax.div(first - first_start + KEY_TILE - 1, KEY_TILE)

        def back(index, carry):
            key_first = pl.multiple_of(first - (index + 1) * KEY_TILE, QUERY_TILE)

            def run(mask):
                fold(scores_of(key_first, KEY_TILE, mask), key_first, KEY_TILE, False)

            either(key_first < last_start, run)
            return carry

        lax.fori_loop(0, steps, back, 0)
        safe = jnp.max(total[...]) < TOTAL_LIMIT

        @pl.when(safe)
        def _():
            store()

        @pl.when(jnp.logical_not(safe))
        def _():
            tile_low = lax.div(first_start, KEY_TILE)
            tile_high = lax.div(last, KEY_TILE) + 1
            top[...] = jnp.full(top.shape, FLOOR, jnp.float32)

            def score(index, carry):
                key_first = pl.multiple_of(index * KEY_TILE, KEY_TILE)
                found = scores_of(key_first, KEY_TILE, True)
                scores[index - tile_low] = found
                best = top[...]
                for c in range(KEY_TILE // 128):
                    best = jnp.maximum(best, found[:, c * 128 : (c + 1) * 128])
                top[...] = best
                return carry

            lax.fori_loop(tile_low, tile_high, score, 0)
            set_top(top[...])
            total[...] = jnp.zeros(total.shape, jnp.float32)
            acc[...] = jnp.zeros(acc.shape, jnp.float32)

            def weigh(index, carry):
                key_first = pl.multiple_of(index * KEY_TILE, KEY_TILE)
                fold(scores[index - tile_low], key_first, KEY_TILE, False)
                return carry

            lax.fori_loop(tile_low, tile_high, weigh, 0)
            store()

        return carry

    lax.fori_loop(0, shard_rows // QUERY_TILE, one_tile, 0)


def attend(lengths, target, keys, query_parts, slots, per_peer, halo):
    sources = len(query_parts)
    part_rows, width = query_parts[0].shape
    shard_rows = part_rows * sources
    rows = (width // HEAD) * QUERY_TILE
    most = (halo * shard_rows) // KEY_TILE + 2
    pairs = shard_rows * 1300 * (width // HEAD)
    return pl.pallas_call(
        functools.partial(attend_kernel, shard_rows, halo, per_peer, sources),
        out_shape=jax.ShapeDtypeStruct((slots, BLOCK, width), jnp.bfloat16),
        in_specs=[SCALARS, SCALARS] + [ANYWHERE] * (4 + sources),
        out_specs=pl.BlockSpec(memory_space=pltpu.VMEM),
        scratch_shapes=[
            pltpu.VMEM(((halo + 1) * shard_rows, 2 * HEAD), jnp.bfloat16),
            pltpu.VMEM((shard_rows, width), jnp.bfloat16),
            pltpu.VMEM((most, rows, KEY_TILE), jnp.float32),
            pltpu.VMEM((rows, 128), jnp.float32),
            pltpu.VMEM((rows, 128), jnp.float32),
            pltpu.VMEM((rows, HEAD), jnp.float32),
            pltpu.SemaphoreType.DMA((3 + sources,)),
        ],
        compiler_params=pltpu.CompilerParams(vmem_limit_bytes=32 << 20),
        cost_estimate=pl.CostEstimate(flops=pairs * 32 * HEAD, bytes_accessed=4 << 20, transcendentals=pairs),
        name="attend",
    )(lengths, target, *keys, *query_parts)


def place_kernel(per_peer, blocks_here, target_ref, *refs):
    pieces, out_ref, sems = refs[:-2], refs[-2], refs[-1]
    shard = lax.axis_index("seq")
    width = pieces[0].shape[2]

    def one(block, carry):
        slot, rank, source, inside = carry
        mine = target_ref[block] == shard

        @pl.when(mine)
        def _():
            for p, piece in enumerate(pieces):
                pltpu.make_async_copy(
                    piece.at[source * per_peer + rank],
                    out_ref.at[pl.ds(pl.multiple_of(slot * BLOCK, BLOCK), BLOCK), pl.ds(p * width, width)],
                    sems.at[p],
                ).start()

        step = mine.astype(jnp.int32)
        ends = inside == blocks_here - 1
        return (
            slot + step,
            jnp.where(ends, 0, rank + step),
            jnp.where(ends, source + 1, source),
            jnp.where(ends, 0, inside + 1),
        )

    zero = jnp.int32(0)
    lax.fori_loop(0, target_ref.shape[0], one, (zero, zero, zero, zero))
    for p in range(len(pieces)):
        landed = out_ref.at[:, pl.ds(p * width, width)]
        pltpu.make_async_copy(landed, landed, sems.at[p]).wait()


def place(target, pieces, out_shape, per_peer):
    return pl.pallas_call(
        functools.partial(place_kernel, per_peer, out_shape[0] // BLOCK),
        out_shape=jax.ShapeDtypeStruct(out_shape, jnp.bfloat16),
        in_specs=[SCALARS] + [ANYWHERE] * len(pieces),
        out_specs=pl.BlockSpec(memory_space=pltpu.VMEM),
        scratch_shapes=[pltpu.SemaphoreType.DMA((len(pieces),))],
        compiler_params=pltpu.CompilerParams(vmem_limit_bytes=16 << 20),
        name="place",
    )(target, *pieces)


def split_keys_kernel(tp, source, *refs):
    outs, held, sems = refs[:-2], refs[-2], refs[-1]
    load = pltpu.make_async_copy(source, held, sems.at[len(outs) * tp])
    load.start()
    load.wait()
    stores = []
    for j, out in enumerate(outs):
        for h in range(tp):
            columns = pl.ds((h * len(outs) + j) * 2 * HEAD, 2 * HEAD)
            stores.append(pltpu.make_async_copy(held.at[:, columns], out.at[h], sems.at[j * tp + h]))
    for copy in stores:
        copy.start()
    for copy in stores:
        copy.wait()


def split_keys(array, tp, count):
    rows = array.shape[0]
    return pl.pallas_call(
        functools.partial(split_keys_kernel, tp),
        out_shape=[jax.ShapeDtypeStruct((tp, rows, 2 * HEAD), array.dtype)] * count,
        in_specs=[ANYWHERE],
        out_specs=[ANYWHERE] * count,
        scratch_shapes=[pltpu.VMEM(array.shape, array.dtype), pltpu.SemaphoreType.DMA((count * tp + 1,))],
        compiler_params=pltpu.CompilerParams(vmem_limit_bytes=16 << 20),
        name="split_keys",
    )(array)


def split_queries_kernel(tp, count, source, *refs):
    outs, held, sems = refs[:-2], refs[-2], refs[-1]
    me = lax.axis_index("tp")
    width = outs[0].shape[1]
    load = pltpu.make_async_copy(source, held, sems.at[len(outs)])
    load.start()
    load.wait()
    stores = []
    for p in range(count):
        for x in range(tp):
            low = pl.multiple_of((me ^ x) * (count * width) + p * width, width)
            place = p * tp + x
            stores.append(pltpu.make_async_copy(held.at[:, pl.ds(low, width)], outs[place], sems.at[place]))
    for copy in stores:
        copy.start()
    for copy in stores:
        copy.wait()


def split_queries(array, tp, count, width):
    rows = array.shape[0]
    total = count * tp
    outs = pl.pallas_call(
        functools.partial(split_queries_kernel, tp, count),
        out_shape=[jax.ShapeDtypeStruct((rows, width), array.dtype)] * total,
        in_specs=[ANYWHERE],
        out_specs=[ANYWHERE] * total,
        scratch_shapes=[pltpu.VMEM(array.shape, array.dtype), pltpu.SemaphoreType.DMA((total + 1,))],
        compiler_params=pltpu.CompilerParams(vmem_limit_bytes=16 << 20),
        name="split_queries",
    )(array)
    return [list(outs[p * tp : (p + 1) * tp]) for p in range(count)]


def after(values, earlier):
    return list(lax.optimization_barrier((tuple(values), tuple(earlier)))[0])


def body(queries, keys_values, doc_lengths, block_target):
    tp = lax.axis_size("tp")
    shards = lax.axis_size("seq")
    shard_rows = queries.shape[0] * tp
    blocks_here = shard_rows // BLOCK
    per_peer = (blocks_here + shards - 1) // shards
    slots = shards * per_peer
    halo = (MAXDOC - 1 + shard_rows - 1) // shard_rows
    kv_here = KV_HEADS // tp
    width = PIECE_HEADS * HEAD
    per_kv = GROUP // PIECE_HEADS
    pieces = kv_here * per_kv
    out_shape = (shard_rows, HEADS * HEAD // tp)

    next_shard = [(i, i + 1) for i in range(shards - 1)]
    next_even = [(i, i + 2) for i in range(0, shards - 2, 2)]
    to_odd = [(i, i + 1) for i in range(2, shards, 2)]

    def gather_keys(part):
        own = lax.all_to_all(part, "tp", split_axis=0, concat_axis=0, tiled=True).reshape(shard_rows, 2 * HEAD)
        near = lax.ppermute(own, "seq", next_shard)
        far_even = lax.ppermute(own, "seq", next_even)
        far_odd = lax.ppermute(near, "seq", to_odd)
        return (far_even, far_odd, near, own)

    def swap(parts):
        return [parts[0]] + [
            lax.ppermute(part, "tp", [(i, i ^ x) for i in range(tp)]) for x, part in enumerate(parts) if x
        ]

    def exchange(piece, parts):
        sent = attend(doc_lengths, block_target, keys[piece // per_kv], parts, slots, per_peer, halo)
        return sent, lax.all_to_all(sent, "seq", split_axis=0, concat_axis=0, tiled=True)

    key_parts = split_keys(keys_values, tp, kv_here)
    query_parts = split_queries(queries, tp, pieces, width)
    keys = [gather_keys(key_parts[0])]
    arrived, sent, received = [None] * pieces, [None] * pieces, [None] * pieces
    for piece in range(pieces):
        parts = query_parts[piece]
        if piece == 1:
            parts = after(parts, keys[0][3:])
        if piece > 1:
            parts = after(parts, arrived[piece - 2][1:])
        if piece > 2:
            parts = after(parts, [sent[piece - 3]])
        arrived[piece] = swap(parts)
        if piece == 0:
            for part in key_parts[1:]:
                keys.append(gather_keys(after([part], keys[0][3:])[0]))
        sent[piece], received[piece] = exchange(piece, arrived[piece])
    return place(block_target, received, out_shape, per_peer)


def solution(mesh):
    placed = (P(("seq", "tp"), None), P(("seq", "tp"), None), P(), P())
    return jax.shard_map(
        body, mesh=mesh, in_specs=placed, out_specs=P("seq", "tp"), check_vma=False
    )
```

time: 373 us -> 255 us (0.68)
  Pallas kernels: 157 us -> 49.9 us
  waiting for transfers between devices: 82.5 us -> 23.6 us
  blocking collectives: 0 us -> 56.2 us
  local copies, waits for them, and re-layouts: 41.1 us -> 14.5 us
  starting transfers between devices: 90.5 us -> 108 us
    pallas_call x4 -> x3, Pallas kernels: 103 us -> 6.13 us  [the longest x1 4.08 us: place(): pl.pallas_call(functools.partial(place_kernel, per_peer, out_shape[0] //...]
    all_to_all x10 -> x4, waiting for transfers between devices: 71.8 us -> 2.7 us  [the longest x3 2.69 us: exchange(): lax.all_to_all(sent, 'seq', split_axis=0, concat_axis=0, tiled=True)]
    all_to_all x0 -> x2, blocking collectives: none -> 56.2 us  [the longest x1 29.7 us: exchange(): lax.all_to_all(sent, 'seq', split_axis=0, concat_axis=0, tiled=True)]
    ppermute x6 -> x18, starting transfers between devices: 14.9 us -> 48.1 us  [the longest x12 34.4 us: swap(): lax.ppermute(part, 'tp', [(i, i ^ x) for i in range(tp)])]
    all_to_all x10 -> x4, starting transfers between devices: 75.6 us -> 59.7 us  [the longest x3 55.5 us: exchange(): lax.all_to_all(sent, 'seq', split_axis=0, concat_axis=0, tiled=True)]
    slice x2 -> x0, local copies, waits for them, and re-layouts: 15 us -> none  [to_heads(): array.reshape(rows, tp, -1, piece_width)[:, :, piece].transpose(1, 0, 2)]
    ppermute x6 -> x18, waiting for transfers between devices: 10.7 us -> 20.9 us  [the longest x12 20.9 us: swap(): lax.ppermute(part, 'tp', [(i, i ^ x) for i in range(tp)])]
    pallas_call x4, Pallas kernels: 54 us -> 43.8 us  [attend(): pl.pallas_call(functools.partial(attend_kernel, shard_rows, halo, per_pee...]
  transfers between devices with their start and end apart: 16 -> 22, of which waited for: 8 -> 4; matrix products, arithmetic and copies ran while one was open for 8% -> 0% of each run, Pallas kernels for 35% -> 18%
where the time goes in v2:
time: 255 us; the launch traced here: 252 us
  starting transfers between devices  108 us (42%)
  blocking collectives  56.2 us (22%)
  Pallas kernels  49.9 us (20%)
  waiting for transfers between devices  23.6 us (9%)
  local copies, waits for them, and re-layouts  14.5 us (6%)
    all_to_all x3, starting transfers between devices, exchange(): lax.all_to_all(sent, 'seq', split_axis=0, concat_axis=0, tiled=True)  55.5 us
    pallas_call x4, Pallas kernels, attend(): pl.pallas_call(functools.partial(attend_kernel, shard_rows, halo, per_pee...  43.8 us
    ppermute x12, starting transfers between devices, swap(): lax.ppermute(part, 'tp', [(i, i ^ x) for i in range(tp)])  34.4 us
    all_to_all x1, blocking collectives, exchange(): lax.all_to_all(sent, 'seq', split_axis=0, concat_axis=0, tiled=True)  29.7 us
    all_to_all x1, blocking collectives, gather_keys(): lax.all_to_all(part, 'tp', split_axis=0, concat_axis=0, tiled=True)  26.5 us
    ppermute x12, waiting for transfers between devices, swap(): lax.ppermute(part, 'tp', [(i, i ^ x) for i in range(tp)])  20.9 us
    unnamed x48, local copies, waits for them, and re-layouts  14.5 us
    ppermute x2, starting transfers between devices, gather_keys(): far_even = lax.ppermute(own, 'seq', next_even)  6.08 us
  transfers between devices with their start and end apart: 22, of which 4 were waited for; matrix products, arithmetic and copies ran while one was open for 0% of the time, Pallas kernels for 18%

profile of v2, /device:TPU:0, one launch (start us, length us, event | category | flops | bytes accessed | tf_op | source)
XLA Modules:
  0.0 252.3 jit_solution(3365683841952717220)
XLA Ops:
  0.0 1.6 copy-done.1
  1.6 0.4 split_keys.1
  2.0 0.0 copy-start.4
  2.0 0.0 copy-start.5
  2.0 0.0 copy-start.23
  2.0 26.5 %all_to_all.30 = bf16[4,384,256]{2,1,0:T(8,128)(2,1)} all-to-all(bf16[4,384,256]{2,1,0:T(8,128)(2,1)S(1)} %get-tuple-element.40), channel_id=1, replica_groups=mesh['seq'=8,'tp'=4] {'tp'}, dimensions={0} | all-to-all | bytes 1572864 | tf_op jit(solution)/shard_map/all_to_all | solution.py:364
  28.5 2.2 collective-permute-start.1
  30.7 4.2 %all-to-all-start.3 = ((bf16[4,384,256]{2,1,0:T(8,128)(2,1)}), bf16[4,384,256]{2,1,0:T(8,128)(2,1)}, u32[]{:S(2)}, u32[]{:S(2)}) async-start(bf16[4,384,256]{2,1,0:T(8,128)(2,1)} %copy-done.4), calls=%async_computation.3 | async-start | bytes 1572864 | tf_op jit(solution)/shard_map/all_to_all | solution.py:364
  34.9 3.2 %collective-permute-start = (bf16[1536,256]{1,0:T(8,128)(2,1)}, bf16[1536,256]{1,0:T(8,128)(2,1)S(1)}, u32[]{:S(2)}, u32[]{:S(2)}) collective-permute-start(bf16[1536,256]{1,0:T(8,128)(2,1)} %bitcast.refs_5_), channel_id=1, source_target_pairs={{0,8},{8,16},{16,24},{1,9},{9,17},{17,25},{2,10},{10,18},{18,26},{... | collective-permute-start | bytes 2359304 | tf_op jit(solution)/shard_map/ppermute | solution.py:366
  38.1 1.6 collective-permute-start.2
  39.7 1.6 split_queries.1
  41.3 0.7 copy-done.11
  42.0 0.7 copy-done.13
  42.7 0.7 copy-done.15
  43.4 2.0 collective-permute-start.3
  45.3 2.4 collective-permute-start.4
  47.7 0.1 collective-permute-start.5
  47.7 4.6 %collective-permute-done.3.refs_7_ = bf16[384,256]{1,0:T(8,128)(2,1)S(1)} collective-permute-done((bf16[384,256]{1,0:T(8,128)(2,1)S(1)}, bf16[384,256]{1,0:T(8,128)(2,1)S(1)}, u32[]{:S(2)}, u32[]{:S(2)}) %collective-permute-start.3) | collective-permute-done | bytes 196640 | tf_op jit(solution)/shard_map/ppermute | solution.py:372
  52.4 2.5 collective-permute-start.6
  54.9 13.8 %collective-permute-done.4.refs_8_ = bf16[384,256]{1,0:T(8,128)(2,1)S(1)} collective-permute-done((bf16[384,256]{1,0:T(8,128)(2,1)S(1)}, bf16[384,256]{1,0:T(8,128)(2,1)S(1)}, u32[]{:S(2)}, u32[]{:S(2)}) %collective-permute-start.4) | collective-permute-done | bytes 196640 | tf_op jit(solution)/shard_map/ppermute | solution.py:372
  68.7 0.0 collective-permute-start.7
  68.7 0.0 collective-permute-done.5.refs_9_
  68.7 1.6 collective-permute-start.8
  70.3 0.0 collective-permute-done.6.refs_7_
  70.3 0.7 copy-done.17
  71.0 12.2 %collective-permute-start.12 = (bf16[384,256]{1,0:T(8,128)(2,1)}, bf16[384,256]{1,0:T(8,128)(2,1)}, u32[]{:S(2)}, u32[]{:S(2)}) collective-permute-start(bf16[384,256]{1,0:T(8,128)(2,1)} %get-tuple-element.60), channel_id=1, source_target_pairs={{0,1},{1,0},{2,3},{3,2},{4,5},{5,4},{6,7},{7,6},{8,9},{9,8},{10,11... | collective-permute-start | bytes 589832 | tf_op jit(solution)/shard_map/ppermute | solution.py:372
  83.2 2.4 collective-permute-done.7.refs_8_
  85.6 0.7 copy-done.19
  86.3 0.0 collective-permute-start.13
  86.3 0.0 collective-permute-done.8.refs_9_
  86.3 0.7 copy-done.21
  87.0 1.5 collective-permute-start.14
  88.5 0.0 collective-permute-done.refs_2_
  88.5 1.0 copy-done.6
  89.4 0.0 all-to-all-done.3
  89.4 2.9 %collective-permute-start.9 = (bf16[1536,256]{1,0:T(8,128)(2,1)}, bf16[1536,256]{1,0:T(8,128)(2,1)S(1)}, u32[]{:S(2)}, u32[]{:S(2)}) collective-permute-start(bf16[1536,256]{1,0:T(8,128)(2,1)} %bitcast.1.refs_5_), channel_id=1, source_target_pairs={{0,8},{8,16},{16,24},{1,9},{9,17},{17,25},{2,10},{10,18},{18,26},{... | collective-permute-start | bytes 2359304 | tf_op jit(solution)/shard_map/ppermute | solution.py:366
  92.3 2.2 collective-permute-start.10
  94.5 1.1 copy-done.7
  95.6 0.9 copy-done.16
  96.6 11.3 %attend.4 = bf16[16,128,256]{2,1,0:T(8,128)(2,1)} custom-call(s32[8]{0:T(128)S(1)} %copy-done.23, s32[96]{0:T(128)S(1)} %copy-done.5, bf16[1536,256]{1,0:T(8,128)(2,1)S(1)} %copy-done.7, bf16[1536,256]{1,0:T(8,128)(2,1)} %collective-permute-done.2.refs_3_, bf16[1536,256]{1,0:T(8,128)(2,1)} %collective-permute-done.1.refs_4_, ...), custom_call_target="tpu_custom_call" | custom-call | flops 16357785600 | bytes 4194304 | tf_op jit(solution)/shard_map/attend/pallas_call | solution.py:212
  107.9 19.8 %all-to-all-start.1 = ((bf16[16,128,256]{2,1,0:T(8,128)(2,1)}), bf16[16,128,256]{2,1,0:T(8,128)(2,1)S(1)}, u32[]{:S(2)}, u32[]{:S(2)}) async-start(bf16[16,128,256]{2,1,0:T(8,128)(2,1)} %attend.4), calls=%async_computation.1 | async-start | bytes 2097152 | tf_op jit(solution)/shard_map/all_to_all | solution.py:377
  127.7 1.7 collective-permute-start.11
  129.4 0.9 copy-done.18
  130.3 0.9 copy-done.20
  131.2 0.9 copy-done.22
  132.2 11.3 %attend.5 = bf16[16,128,256]{2,1,0:T(8,128)(2,1)} custom-call(s32[8]{0:T(128)S(1)} %copy-done.23, s32[96]{0:T(128)S(1)} %copy-done.5, bf16[1536,256]{1,0:T(8,128)(2,1)S(1)} %copy-done.8, bf16[1536,256]{1,0:T(8,128)(2,1)} %collective-permute-done.2.refs_3_, bf16[1536,256]{1,0:T(8,128)(2,1)} %collective-permute-done.1.refs_4_, ...), custom_call_target="tpu_custom_call" | custom-call | flops 16357785600 | bytes 4194304 | tf_op jit(solution)/shard_map/attend/pallas_call | solution.py:212
  143.5 18.5 %all-to-all-start.2 = ((bf16[16,128,256]{2,1,0:T(8,128)(2,1)}), bf16[16,128,256]{2,1,0:T(8,128)(2,1)S(1)}, u32[]{:S(2)}, u32[]{:S(2)}) async-start(bf16[16,128,256]{2,1,0:T(8,128)(2,1)} %attend.5), calls=%async_computation.2 | async-start | bytes 2097152 | tf_op jit(solution)/shard_map/all_to_all | solution.py:377
  162.0 0.0 collective-permute-done.12.refs_7_
  162.0 4.2 %collective-permute-start.15 = (bf16[384,256]{1,0:T(8,128)(2,1)}, bf16[384,256]{1,0:T(8,128)(2,1)}, u32[]{:S(2)}, u32[]{:S(2)}) collective-permute-start(bf16[384,256]{1,0:T(8,128)(2,1)} %get-tuple-element.72), channel_id=1, source_target_pairs={{0,1},{1,0},{2,3},{3,2},{4,5},{5,4},{6,7},{7,6},{8,9},{9,8},{10,11... | collective-permute-start | bytes 589832 | tf_op jit(solution)/shard_map/ppermute | solution.py:372
  166.1 6.5 %collective-permute-start.16 = (bf16[384,256]{1,0:T(8,128)(2,1)}, bf16[384,256]{1,0:T(8,128)(2,1)}, u32[]{:S(2)}, u32[]{:S(2)}) collective-permute-start(bf16[384,256]{1,0:T(8,128)(2,1)} %get-tuple-element.73), channel_id=1, source_target_pairs={{0,2},{1,3},{2,0},{3,1},{4,6},{5,7},{6,4},{7,5},{8,10},{9,11},{10,... | collective-permute-start | bytes 589832 | tf_op jit(solution)/shard_map/ppermute | solution.py:372
  172.7 0.0 collective-permute-done.14.refs_9_
  172.7 1.4 collective-permute-start.17
  174.1 0.0 collective-permute-done.9.refs_2_
  174.1 0.0 collective-permute-done.11.refs_3_
  174.2 10.6 %attend.6 = bf16[16,128,256]{2,1,0:T(8,128)(2,1)S(1)} custom-call(s32[8]{0:T(128)S(1)} %copy-done.23, s32[96]{0:T(128)S(1)} %copy-done.5, bf16[1536,256]{1,0:T(8,128)(2,1)S(1)} %collective-permute-done.9.refs_2_, bf16[1536,256]{1,0:T(8,128)(2,1)} %collective-permute-done.11.refs_3_, bf16[1536,256]{1,0:T(8,128)(2,1)} %collective-permute-done.10.refs_4_, ...), custom_call_target="tpu_custom_call" | custom-call | flops 16357785600 | bytes 4194304 | tf_op jit(solution)/shard_map/attend/pallas_call | solution.py:212
  184.7 0.0 copy-start.2
  184.8 1.0 copy-done.2
  185.7 17.3 %all-to-all-start.4 = ((bf16[16,128,256]{2,1,0:T(8,128)(2,1)}), bf16[16,128,256]{2,1,0:T(8,128)(2,1)S(1)}, u32[]{:S(2)}, u32[]{:S(2)}) async-start(bf16[16,128,256]{2,1,0:T(8,128)(2,1)} %copy-done.2), calls=%async_computation.4 | async-start | bytes 2097152 | tf_op jit(solution)/shard_map/all_to_all | solution.py:377
  203.1 1.1 copy-done.10
  204.2 10.6 %attend.7 = bf16[16,128,256]{2,1,0:T(8,128)(2,1)S(1)} custom-call(s32[8]{0:T(128)S(1)} %copy-done.23, s32[96]{0:T(128)S(1)} %copy-done.5, bf16[1536,256]{1,0:T(8,128)(2,1)S(1)} %copy-done.10, bf16[1536,256]{1,0:T(8,128)(2,1)} %collective-permute-done.11.refs_3_, bf16[1536,256]{1,0:T(8,128)(2,1)} %collective-permute-done.10.refs_4_, ...), custom_call_target="tpu_custom_call" | custom-call | flops 16357785600 | bytes 4194304 | tf_op jit(solution)/shard_map/attend/pallas_call | solution.py:212
  214.8 1.0 copy-done.3
  215.8 2.7 %all-to-all-done.4.refs_2_ = bf16[16,128,256]{2,1,0:T(8,128)(2,1)S(1)} async-done(((bf16[16,128,256]{2,1,0:T(8,128)(2,1)}), bf16[16,128,256]{2,1,0:T(8,128)(2,1)S(1)}, u32[]{:S(2)}, u32[]{:S(2)}) %all-to-all-start.4) | async-done | bytes 1048608 | tf_op jit(solution)/shard_map/all_to_all | solution.py:377
  218.5 29.7 %all_to_all.31.refs_3_ = bf16[16,128,256]{2,1,0:T(8,128)(2,1)S(1)} all-to-all(bf16[16,128,256]{2,1,0:T(8,128)(2,1)} %copy-done.3), channel_id=1, replica_groups=mesh['seq'=8,'tp'=4] {'seq'}, dimensions={0} | all-to-all | bytes 2097152 | tf_op jit(solution)/shard_map/all_to_all | solution.py:377
  248.2 4.1 %place.1 = bf16[1536,1024]{1,0:T(8,128)(2,1)} custom-call(s32[96]{0:T(128)S(1)} %copy-done.5, bf16[16,128,256]{2,1,0:T(8,128)(2,1)S(1)} %all-to-all-done.1.refs_0_, bf16[16,128,256]{2,1,0:T(8,128)(2,1)S(1)} %all-to-all-done.2.refs_1_, bf16[16,128,256]{2,1,0:T(8,128)(2,1)S(1)} %all-to-all-done.4.refs_2_, bf16[16,128,256]{2,1,0:T(8,128)(2,1)S(1)} %all_to_all.31.refs_3_), custom_call_target="tpu_custom_call" | custom-call | tf_op jit(solution)/shard_map/place/pallas_call | solution.py:267
  (37 shorter events, 0.1 us)
Async XLA Ops:
  0.0 39.7 %copy-start = (bf16[384,4096]{1,0:T(8,128)(2,1)S(1)}, bf16[384,4096]{1,0:T(8,128)(2,1)}, u32[]{:S(2)}) copy-start(bf16[384,4096]{1,0:T(8,128)(2,1)} %source.3) | copy-start | bytes 9437188
  0.0 1.6 copy-start.1
  2.0 28.7 %copy-start.4 = (bf16[4,384,256]{2,1,0:T(8,128)(2,1)}, bf16[4,384,256]{2,1,0:T(8,128)(2,1)S(1)}, u32[]{:S(2)}) copy-start(bf16[4,384,256]{2,1,0:T(8,128)(2,1)S(1)} %get-tuple-element.54) | copy-start | bytes 2359300
  2.0 92.5 %copy-start.5 = (s32[96]{0:T(128)S(1)}, s32[96]{0:T(128)}, u32[]{:S(2)}) copy-start(s32[96]{0:T(128)} %target_ref.1) | copy-start | bytes 1156
  2.0 92.5 %copy-start.23 = (s32[8]{0:T(128)S(1)}, s32[8]{0:T(128)}, u32[]{:S(2)}) copy-start(s32[8]{0:T(128)} %refs_0_.7) | copy-start | bytes 100
  28.5 9.6 %collective-permute-start.1 = (bf16[1536,256]{1,0:T(8,128)(2,1)}, bf16[1536,256]{1,0:T(8,128)(2,1)}, u32[]{:S(2)}, u32[]{:S(2)}) collective-permute-start(bf16[1536,256]{1,0:T(8,128)(2,1)} %bitcast.refs_5_), channel_id=1, source_target_pairs={{0,4},{4,8},{8,12},{12,16},{16,20},{20,24},{24,28},{1,5},{5,9},{9,... | collective-permute-start | bytes 2359304 | tf_op jit(solution)/shard_map/ppermute | solution.py:365
  30.7 58.8 %all-to-all-start.3 = ((bf16[4,384,256]{2,1,0:T(8,128)(2,1)}), bf16[4,384,256]{2,1,0:T(8,128)(2,1)}, u32[]{:S(2)}, u32[]{:S(2)}) async-start(bf16[4,384,256]{2,1,0:T(8,128)(2,1)} %copy-done.4), calls=%async_computation.3 | async-start | bytes 1572864 | tf_op jit(solution)/shard_map/all_to_all | solution.py:364
  34.9 53.6 %collective-permute-start = (bf16[1536,256]{1,0:T(8,128)(2,1)}, bf16[1536,256]{1,0:T(8,128)(2,1)S(1)}, u32[]{:S(2)}, u32[]{:S(2)}) collective-permute-start(bf16[1536,256]{1,0:T(8,128)(2,1)} %bitcast.refs_5_), channel_id=1, source_target_pairs={{0,8},{8,16},{16,24},{1,9},{9,17},{17,25},{2,10},{10,18},{18,26},{... | collective-permute-start | bytes 2359304 | tf_op jit(solution)/shard_map/ppermute | solution.py:366
  38.1 54.2 %collective-permute-start.2 = (bf16[1536,256]{1,0:T(8,128)(2,1)}, bf16[1536,256]{1,0:T(8,128)(2,1)}, u32[]{:S(2)}, u32[]{:S(2)}) collective-permute-start(bf16[1536,256]{1,0:T(8,128)(2,1)} %collective-permute-done.1.refs_4_), channel_id=1, source_target_pairs={{8,12},{16,20},{24,28},{9,13},{17,21},{25,29},{10,14},{18,22},{26,... | collective-permute-start | bytes 2359304 | tf_op jit(solution)/shard_map/ppermute | solution.py:367
  41.3 0.7 copy-start.11
  42.0 0.7 copy-start.13
  42.7 0.7 copy-start.15
  43.4 9.0 %collective-permute-start.3 = (bf16[384,256]{1,0:T(8,128)(2,1)S(1)}, bf16[384,256]{1,0:T(8,128)(2,1)S(1)}, u32[]{:S(2)}, u32[]{:S(2)}) collective-permute-start(bf16[384,256]{1,0:T(8,128)(2,1)S(1)} %get-tuple-element.42), channel_id=1, source_target_pairs={{0,1},{1,0},{2,3},{3,2},{4,5},{5,4},{6,7},{7,6},{8,9},{9,8},{10,11... | collective-permute-start | bytes 589832 | tf_op jit(solution)/shard_map/ppermute | solution.py:372
  45.3 23.3 %collective-permute-start.4 = (bf16[384,256]{1,0:T(8,128)(2,1)S(1)}, bf16[384,256]{1,0:T(8,128)(2,1)S(1)}, u32[]{:S(2)}, u32[]{:S(2)}) collective-permute-start(bf16[384,256]{1,0:T(8,128)(2,1)S(1)} %get-tuple-element.43), channel_id=1, source_target_pairs={{0,2},{1,3},{2,0},{3,1},{4,6},{5,7},{6,4},{7,5},{8,10},{9,11},{10,... | collective-permute-start | bytes 589832 | tf_op jit(solution)/shard_map/ppermute | solution.py:372
  47.7 21.0 %collective-permute-start.5 = (bf16[384,256]{1,0:T(8,128)(2,1)S(1)}, bf16[384,256]{1,0:T(8,128)(2,1)S(1)}, u32[]{:S(2)}, u32[]{:S(2)}) collective-permute-start(bf16[384,256]{1,0:T(8,128)(2,1)S(1)} %get-tuple-element.44), channel_id=1, source_target_pairs={{0,3},{1,2},{2,1},{3,0},{4,7},{5,6},{6,5},{7,4},{8,11},{9,10},{10,... | collective-permute-start | bytes 589832 | tf_op jit(solution)/shard_map/ppermute | solution.py:372
  52.4 17.9 %collective-permute-start.6 = (bf16[384,256]{1,0:T(8,128)(2,1)S(1)}, bf16[384,256]{1,0:T(8,128)(2,1)S(1)}, u32[]{:S(2)}, u32[]{:S(2)}) collective-permute-start(bf16[384,256]{1,0:T(8,128)(2,1)S(1)} %get-tuple-element.50), channel_id=1, source_target_pairs={{0,1},{1,0},{2,3},{3,2},{4,5},{5,4},{6,7},{7,6},{8,9},{9,8},{10,11... | collective-permute-start | bytes 589832 | tf_op jit(solution)/shard_map/ppermute | solution.py:372
  68.7 17.0 %collective-permute-start.7 = (bf16[384,256]{1,0:T(8,128)(2,1)S(1)}, bf16[384,256]{1,0:T(8,128)(2,1)S(1)}, u32[]{:S(2)}, u32[]{:S(2)}) collective-permute-start(bf16[384,256]{1,0:T(8,128)(2,1)S(1)} %get-tuple-element.51), channel_id=1, source_target_pairs={{0,2},{1,3},{2,0},{3,1},{4,6},{5,7},{6,4},{7,5},{8,10},{9,11},{10,... | collective-permute-start | bytes 589832 | tf_op jit(solution)/shard_map/ppermute | solution.py:372
  68.7 17.6 %collective-permute-start.8 = (bf16[384,256]{1,0:T(8,128)(2,1)S(1)}, bf16[384,256]{1,0:T(8,128)(2,1)S(1)}, u32[]{:S(2)}, u32[]{:S(2)}) collective-permute-start(bf16[384,256]{1,0:T(8,128)(2,1)S(1)} %get-tuple-element.52), channel_id=1, source_target_pairs={{0,3},{1,2},{2,1},{3,0},{4,7},{5,6},{6,5},{7,4},{8,11},{9,10},{10,... | collective-permute-start | bytes 589832 | tf_op jit(solution)/shard_map/ppermute | solution.py:372
  70.3 0.7 copy-start.17
  71.0 91.0 %collective-permute-start.12 = (bf16[384,256]{1,0:T(8,128)(2,1)}, bf16[384,256]{1,0:T(8,128)(2,1)}, u32[]{:S(2)}, u32[]{:S(2)}) collective-permute-start(bf16[384,256]{1,0:T(8,128)(2,1)} %get-tuple-element.60), channel_id=1, source_target_pairs={{0,1},{1,0},{2,3},{3,2},{4,5},{5,4},{6,7},{7,6},{8,9},{9,8},{10,11... | collective-permute-start | bytes 589832 | tf_op jit(solution)/shard_map/ppermute | solution.py:372
  85.6 0.7 copy-start.19
  86.3 79.8 %collective-permute-start.13 = (bf16[384,256]{1,0:T(8,128)(2,1)}, bf16[384,256]{1,0:T(8,128)(2,1)}, u32[]{:S(2)}, u32[]{:S(2)}) collective-permute-start(bf16[384,256]{1,0:T(8,128)(2,1)} %get-tuple-element.61), channel_id=1, source_target_pairs={{0,2},{1,3},{2,0},{3,1},{4,6},{5,7},{6,4},{7,5},{8,10},{9,11},{10,... | collective-permute-start | bytes 589832 | tf_op jit(solution)/shard_map/ppermute | solution.py:372
  86.3 0.7 copy-start.21
  87.0 85.7 %collective-permute-start.14 = (bf16[384,256]{1,0:T(8,128)(2,1)}, bf16[384,256]{1,0:T(8,128)(2,1)}, u32[]{:S(2)}, u32[]{:S(2)}) collective-permute-start(bf16[384,256]{1,0:T(8,128)(2,1)} %get-tuple-element.62), channel_id=1, source_target_pairs={{0,3},{1,2},{2,1},{3,0},{4,7},{5,6},{6,5},{7,4},{8,11},{9,10},{10,... | collective-permute-start | bytes 589832 | tf_op jit(solution)/shard_map/ppermute | solution.py:372
  88.5 1.0 copy-start.6
  89.4 84.7 %collective-permute-start.9 = (bf16[1536,256]{1,0:T(8,128)(2,1)}, bf16[1536,256]{1,0:T(8,128)(2,1)S(1)}, u32[]{:S(2)}, u32[]{:S(2)}) collective-permute-start(bf16[1536,256]{1,0:T(8,128)(2,1)} %bitcast.1.refs_5_), channel_id=1, source_target_pairs={{0,8},{8,16},{16,24},{1,9},{9,17},{17,25},{2,10},{10,18},{18,26},{... | collective-permute-start | bytes 2359304 | tf_op jit(solution)/shard_map/ppermute | solution.py:366
  92.3 35.4 %collective-permute-start.10 = (bf16[1536,256]{1,0:T(8,128)(2,1)}, bf16[1536,256]{1,0:T(8,128)(2,1)}, u32[]{:S(2)}, u32[]{:S(2)}) collective-permute-start(bf16[1536,256]{1,0:T(8,128)(2,1)} %bitcast.1.refs_5_), channel_id=1, source_target_pairs={{0,4},{4,8},{8,12},{12,16},{16,20},{20,24},{24,28},{1,5},{5,9},{9,... | collective-permute-start | bytes 2359304 | tf_op jit(solution)/shard_map/ppermute | solution.py:365
  94.5 1.1 copy-start.7
  95.6 0.9 copy-start.16
  96.6 32.8 %copy-start.8 = (bf16[1536,256]{1,0:T(8,128)(2,1)S(1)}, bf16[1536,256]{1,0:T(8,128)(2,1)}, u32[]{:S(2)}) copy-start(bf16[1536,256]{1,0:T(8,128)(2,1)} %copy-done.6) | copy-start | bytes 2359300
  96.6 32.8 %copy-start.14 = (bf16[384,256]{1,0:T(8,128)(2,1)S(1)}, bf16[384,256]{1,0:T(8,128)(2,1)}, u32[]{:S(2)}) copy-start(bf16[384,256]{1,0:T(8,128)(2,1)} %copy-done.13) | copy-start | bytes 589828
  107.9 35.6 %all-to-all-start.1 = ((bf16[16,128,256]{2,1,0:T(8,128)(2,1)}), bf16[16,128,256]{2,1,0:T(8,128)(2,1)S(1)}, u32[]{:S(2)}, u32[]{:S(2)}) async-start(bf16[16,128,256]{2,1,0:T(8,128)(2,1)} %attend.4), calls=%async_computation.1 | async-start | bytes 2097152 | tf_op jit(solution)/shard_map/all_to_all | solution.py:377
  127.7 46.5 %copy-start.12 = (bf16[384,256]{1,0:T(8,128)(2,1)S(1)}, bf16[384,256]{1,0:T(8,128)(2,1)}, u32[]{:S(2)}) copy-start(bf16[384,256]{1,0:T(8,128)(2,1)} %copy-done.11) | copy-start | bytes 589828
  127.7 46.5 %collective-permute-start.11 = (bf16[1536,256]{1,0:T(8,128)(2,1)}, bf16[1536,256]{1,0:T(8,128)(2,1)}, u32[]{:S(2)}, u32[]{:S(2)}) collective-permute-start(bf16[1536,256]{1,0:T(8,128)(2,1)} %collective-permute-done.10.refs_4_), channel_id=1, source_target_pairs={{8,12},{16,20},{24,28},{9,13},{17,21},{25,29},{10,14},{18,22},{26,... | collective-permute-start | bytes 2359304 | tf_op jit(solution)/shard_map/ppermute | solution.py:367
  129.4 0.9 copy-start.18
  130.3 0.9 copy-start.20
  131.2 0.9 copy-start.22
  143.5 42.2 %all-to-all-start.2 = ((bf16[16,128,256]{2,1,0:T(8,128)(2,1)}), bf16[16,128,256]{2,1,0:T(8,128)(2,1)S(1)}, u32[]{:S(2)}, u32[]{:S(2)}) async-start(bf16[16,128,256]{2,1,0:T(8,128)(2,1)} %attend.5), calls=%async_computation.2 | async-start | bytes 2097152 | tf_op jit(solution)/shard_map/all_to_all | solution.py:377
  162.0 41.1 %collective-permute-start.15 = (bf16[384,256]{1,0:T(8,128)(2,1)}, bf16[384,256]{1,0:T(8,128)(2,1)}, u32[]{:S(2)}, u32[]{:S(2)}) collective-permute-start(bf16[384,256]{1,0:T(8,128)(2,1)} %get-tuple-element.72), channel_id=1, source_target_pairs={{0,1},{1,0},{2,3},{3,2},{4,5},{5,4},{6,7},{7,6},{8,9},{9,8},{10,11... | collective-permute-start | bytes 589832 | tf_op jit(solution)/shard_map/ppermute | solution.py:372
  166.1 36.9 %collective-permute-start.16 = (bf16[384,256]{1,0:T(8,128)(2,1)}, bf16[384,256]{1,0:T(8,128)(2,1)}, u32[]{:S(2)}, u32[]{:S(2)}) collective-permute-start(bf16[384,256]{1,0:T(8,128)(2,1)} %get-tuple-element.73), channel_id=1, source_target_pairs={{0,2},{1,3},{2,0},{3,1},{4,6},{5,7},{6,4},{7,5},{8,10},{9,11},{10,... | collective-permute-start | bytes 589832 | tf_op jit(solution)/shard_map/ppermute | solution.py:372
  172.7 30.4 %collective-permute-start.17 = (bf16[384,256]{1,0:T(8,128)(2,1)S(1)}, bf16[384,256]{1,0:T(8,128)(2,1)}, u32[]{:S(2)}, u32[]{:S(2)}) collective-permute-start(bf16[384,256]{1,0:T(8,128)(2,1)S(1)} %get-tuple-element.74), channel_id=1, source_target_pairs={{0,3},{1,2},{2,1},{3,0},{4,7},{5,6},{6,5},{7,4},{8,11},{9,10},{10,... | collective-permute-start | bytes 589832 | tf_op jit(solution)/shard_map/ppermute | solution.py:372
  174.1 10.6 %copy-start.9 = (bf16[1536,256]{1,0:T(8,128)(2,1)}, bf16[1536,256]{1,0:T(8,128)(2,1)S(1)}, u32[]{:S(2)}) copy-start(bf16[1536,256]{1,0:T(8,128)(2,1)S(1)} %collective-permute-done.9.refs_2_) | copy-start | bytes 2359300
  184.7 1.0 copy-start.2
  185.7 32.7 %all-to-all-start.4 = ((bf16[16,128,256]{2,1,0:T(8,128)(2,1)}), bf16[16,128,256]{2,1,0:T(8,128)(2,1)S(1)}, u32[]{:S(2)}, u32[]{:S(2)}) async-start(bf16[16,128,256]{2,1,0:T(8,128)(2,1)} %copy-done.2), calls=%async_computation.4 | async-start | bytes 2097152 | tf_op jit(solution)/shard_map/all_to_all | solution.py:377
  203.1 1.1 copy-start.10
  214.8 1.0 copy-start.3
